TPU v7x, 32 devices: a whole 2x2x4 slice. The times are simulated.
32 devices in a mesh: dp: 16 (over z, x, core), fsdp: 2 (over y).
Axes of the slice: x: 2, y: 2, z: 4, core: 2. Of those that a mesh axis runs over, the one named last changes fastest.
Arguments:
- tokens: bfloat16 [6144, 6144], P(('dp', 'fsdp')), may hold values from -6 to 6
- cotangent: bfloat16 [6144, 6144], P(('dp', 'fsdp')), may hold values from -6 to 6
- lengths: int32 [32, 3], P(('dp', 'fsdp')), may hold values from 0 to 80, as said below
- positions: int32 [2, 6144], P(None, ('dp', 'fsdp')), may hold values from 0 to 63, as said below
- weights: bfloat16 [4, 6144, 256], P(None, 'fsdp'), may hold values from -0.078125 to 0.078125
Outputs:
- grad_tokens: bfloat16 [6144, 6144], P(('dp', 'fsdp'))
- weight_grads: float32 [4, 6144, 256], P(None, 'fsdp')
Inputs may be any that keep to these rules, and one draw needn't show every extreme that they name: Devices pair up: dp indices i and i + 8 with the same fsdp index. In every pair exactly one device holds more than 112 live patches; its third image is not empty, its first two images together hold at most 112 patches, and its partner's live patches plus that third image are at most 112. No device holds more than 192 live patches; the first pair's heavy device holds exactly 192. Every non-empty image has at least 10 patches; lengths are 0 only in the light device's third slot. `positions`: each image is laid out row by row with a width w of 2 to 64 patches (exactly 64 for images of 80 patches): its patch number k has row k // w and column k % w; padding rows hold 0.
All inputs are finite; a program needn't handle non-finite values.
Results may differ from a plain program's by a relative error of at most 0.015.
Values may be sent and summed in bfloat16 or wider, within the bound.
A program may use at most 128 MiB of HBM per device.

v0:
```python
import functools
import math

import jax
import jax.numpy as jnp
from jax import lax
from jax.experimental import pallas as pl
from jax.experimental.pallas import tpu as pltpu
from jax.sharding import PartitionSpec as P

HD = 128
TILE = 256


rope_base = 100.0


def layer_norm(values):
    center = values - jnp.mean(values, axis=-1, keepdims=True)
    return center * lax.rsqrt(jnp.mean(center * center, axis=-1, keepdims=True) + 1e-06)


def rotate(values, row_index, col_index):
    quarter = values.shape[-1] // 4
    frequency = rope_base ** (-jnp.arange(quarter, dtype=jnp.float32) / quarter)
    pieces = []
    for offset, where_at in ((0, row_index), (2 * quarter, col_index)):
        angles = where_at.astype(jnp.float32)[:, None, None] * frequency[None, None, :]
        cosine = jnp.cos(angles)
        sine_part = jnp.sin(angles)
        first_half = values[..., offset : offset + quarter]
        second = values[..., offset + quarter : offset + 2 * quarter]
        pieces.append(first_half * cosine - second * sine_part)
        pieces.append(second * cosine + first_half * sine_part)
    return jnp.concatenate(pieces, axis=-1)


def segment_ids(image_lengths, row_count):
    image_ends = jnp.cumsum(image_lengths)
    row_index = jnp.arange(row_count, dtype=jnp.int32)
    slot_number = jnp.sum((row_index[:, None] >= image_ends[None, :]).astype(jnp.int32), axis=1)
    return jnp.where(slot_number < image_lengths.shape[0], slot_number, -1)


def attend(query_lin, key_lin, value_lin, row_index, col_index, segment):
    row_count = query_lin.shape[0]
    score_scale = 1.0 / math.sqrt(HD)
    queries = rotate(layer_norm(query_lin.reshape(row_count, -1, HD)), row_index, col_index).astype(
        jnp.bfloat16
    )
    keys_rot = rotate(layer_norm(key_lin.reshape(row_count, -1, HD)), row_index, col_index).astype(
        jnp.bfloat16
    )
    values = value_lin.reshape(row_count, -1, HD).astype(jnp.bfloat16)
    scores = (
        jnp.einsum("qhd,khd->hqk", queries.astype(jnp.float32), keys_rot.astype(jnp.float32))
        * score_scale
    )
    same = (segment[:, None] == segment[None, :])[None, :, :]
    exponent = jnp.where(same, jnp.exp(scores), jnp.float32(0.0))
    probabilities = (exponent / jnp.sum(exponent, axis=-1, keepdims=True)).astype(jnp.bfloat16)
    attended = jnp.einsum(
        "hqk,khd->qhd", probabilities.astype(jnp.float32), values.astype(jnp.float32)
    ).astype(jnp.bfloat16)
    return attended.reshape(row_count, -1)


def shifted(value, offset):
    count = lax.axis_size("fsdp")
    return lax.ppermute(value, "fsdp", [(i, (i + offset) % count) for i in range(count)])


def part_of(values, index, width):
    return lax.dynamic_slice_in_dim(values, index * width, width, axis=1)


def sum_kernel(orders, slab, head_size, lhs_ref, small_ref, out_ref, acc, outgoing, incoming, send_sem, recv_sem):
    me = lax.axis_index("dp")
    streams, steps = len(orders), len(orders[0])
    rows = 4 * slab // streams
    halves = [rows >> (s + 1) for s in range(steps)]
    starts = [rows - 2 * halves[s] for s in range(steps)]
    bit_of = [(me // (1 << bit)) % 2 for bit in range(steps)]
    peer_of = [me + (1 - 2 * bit_of[bit]) * (1 << bit) for bit in range(steps)]

    barrier = pltpu.get_barrier_semaphore()
    for bit in range(steps):
        pl.semaphore_signal(barrier, inc=1, device_id={"dp": peer_of[bit]}, device_id_type=pl.DeviceIdType.MESH)
    pl.semaphore_wait(barrier, steps)

    def term(stream, row):
        row = stream * rows + row
        weight = row // slab
        left = pl.multiple_of((weight // 3) * slab + row % slab, TILE)
        column = pl.multiple_of(weight * head_size, head_size)
        return jnp.dot(
            lhs_ref[pl.ds(left, TILE), :],
            small_ref[:, pl.ds(column, head_size)],
            preferred_element_type=jnp.float32,
        )

    def exchange(phase, stream, step, source, target):
        copy = pltpu.make_async_remote_copy(
            src_ref=source,
            dst_ref=target,
            send_sem=send_sem.at[phase, stream, step],
            recv_sem=recv_sem.at[phase, stream, step],
            device_id={"dp": peer_of[orders[stream][step]]},
            device_id_type=pl.DeviceIdType.MESH,
        )
        copy.start()
        return copy

    copies = {}
    offsets = {}
    for stream in range(streams):
        half = halves[0]
        mine = bit_of[orders[stream][0]]

        @pl.loop(0, half // TILE)
        def leaving(t):
            value = term(stream, (1 - mine) * half + t * TILE)
            outgoing[stream, pl.ds(pl.multiple_of(t * TILE, TILE), TILE), :] = value.astype(jnp.bfloat16)

        copies[0, stream, 0] = exchange(
            0, stream, 0, outgoing.at[stream, pl.ds(0, half)], incoming.at[stream, pl.ds(0, half)]
        )
        offsets[stream, 0] = mine * half

    for stream in range(streams):
        half = halves[0]
        mine = bit_of[orders[stream][0]]

        @pl.loop(0, half // TILE)
        def kept(t):
            acc[stream, pl.ds(pl.multiple_of(t * TILE, TILE), TILE), :] = term(stream, mine * half + t * TILE)

    for step in range(1, steps + 1):
        for stream in range(streams):
            copies[0, stream, step - 1].wait_recv()
            got = starts[step - 1]
            base = offsets[stream, step - 1] - offsets[stream, 0]
            if step < steps:
                half = halves[step]
                size = min(half, 192)
                mine = bit_of[orders[stream][step]]
                go, stay = (1 - mine) * half, mine * half

                @pl.loop(0, half // size)
                def leaving(t):
                    at = pl.multiple_of(t * size, size)
                    value = acc[stream, pl.ds(pl.multiple_of(base + go + at, size), size), :]
                    other = incoming[stream, pl.ds(pl.multiple_of(got + go + at, size), size), :]
                    outgoing[stream, pl.ds(pl.multiple_of(starts[step] + at, size), size), :] = (
                        value + other.astype(jnp.float32)
                    ).astype(jnp.bfloat16)

                place = pl.ds(starts[step], half)
                copies[0, stream, step] = exchange(
                    0, stream, step, outgoing.at[stream, place], incoming.at[stream, place]
                )

                @pl.loop(0, half // size)
                def kept(t):
                    at = pl.multiple_of(t * size, size)
                    where = pl.ds(pl.multiple_of(base + stay + at, size), size)
                    other = incoming[stream, pl.ds(pl.multiple_of(got + stay + at, size), size), :]
                    acc[stream, where, :] = acc[stream, where, :] + other.astype(jnp.float32)

                offsets[stream, step] = offsets[stream, step - 1] + stay
            else:
                half = halves[steps - 1]
                place = pl.ds(pl.multiple_of(stream * rows + offsets[stream, steps - 1], half), half)
                value = acc[stream, pl.ds(pl.multiple_of(base, half), half), :]
                other = incoming[stream, pl.ds(got, half), :]
                out_ref[place, :] = (value + other.astype(jnp.float32)).astype(jnp.bfloat16)
                copies[1, stream, steps - 1] = exchange(
                    1, stream, steps - 1, out_ref.at[place], out_ref.at[place]
                )

    for step in reversed(range(steps - 1)):
        for stream in range(streams):
            copies[1, stream, step + 1].wait_recv()
            half = halves[step]
            place = pl.ds(pl.multiple_of(stream * rows + offsets[stream, step], half), half)
            copies[1, stream, step] = exchange(1, stream, step, out_ref.at[place], out_ref.at[place])
    for stream in range(streams):
        copies[1, stream, 0].wait_recv()
    for copy in copies.values():
        copy.wait_send()


def summed_terms(lhs, small, slab, head_size):
    steps = lax.axis_size("dp").bit_length() - 1
    streams = 4 if (slab >> steps) % 16 == 0 else 2
    rows = 4 * slab // streams
    plain = list(range(steps))
    turned = plain[:1] + plain[2:] + plain[1:2]
    orders = [turned] + [plain] * (streams - 1)
    moved = rows - (rows >> steps)
    return pl.pallas_call(
        functools.partial(sum_kernel, orders, slab, head_size),
        out_shape=jax.ShapeDtypeStruct((4 * slab, head_size), jnp.bfloat16),
        in_specs=[pl.BlockSpec(memory_space=pltpu.VMEM)] * 2,
        out_specs=pl.BlockSpec(memory_space=pltpu.VMEM),
        scratch_shapes=[
            pltpu.VMEM((streams, rows // 2, head_size), jnp.float32),
            pltpu.VMEM((streams, moved, head_size), jnp.bfloat16),
            pltpu.VMEM((streams, moved, head_size), jnp.bfloat16),
            pltpu.SemaphoreType.DMA((2, streams, steps)),
            pltpu.SemaphoreType.DMA((2, streams, steps)),
        ],
        compiler_params=pltpu.CompilerParams(
            collective_id=0, has_side_effects=True, vmem_limit_bytes=48 * 1024 * 1024
        ),
        cost_estimate=pl.CostEstimate(flops=10**9, bytes_accessed=10**8, transcendentals=0),
    )(lhs, small)


def per_device(tokens, cotangent, lengths, positions, weights):
    capacity = tokens.shape[0]
    slab = weights.shape[1]
    head_size = weights.shape[-1]
    count = lax.axis_size("fsdp")
    me = lax.axis_index("fsdp")
    segment = segment_ids(lengths[0], capacity)
    grad_out = jnp.where((segment >= 0)[:, None], cotangent, jnp.zeros_like(cotangent))
    source = tokens.astype(jnp.float32)
    normed = layer_norm(source).astype(jnp.bfloat16)

    grad_parts = [part_of(grad_out, me, slab)]
    norm_parts = [part_of(normed, me, slab)]
    for k in range(1, count):
        peer = (me + k) % count
        grad_parts.append(shifted(part_of(grad_out, peer, slab), k))
        norm_parts.append(shifted(part_of(normed, peer, slab), k))

    def products(norm_part, grad_part):
        pieces = [jnp.dot(norm_part, weights[i], preferred_element_type=jnp.float32) for i in range(3)]
        pieces.append(jnp.dot(grad_part, weights[3], preferred_element_type=jnp.float32))
        return jnp.concatenate(pieces, axis=1)

    linear = products(norm_parts[0], grad_parts[0])
    for k in range(1, count):
        partial = products(norm_parts[k], grad_parts[k]).astype(jnp.bfloat16)
        linear = linear + shifted(partial, -k).astype(jnp.float32)
    grad_attn = linear[:, 3 * head_size :].astype(jnp.bfloat16)

    def core(query_in, key_in, value_in):
        return attend(query_in, key_in, value_in, positions[0], positions[1], segment)

    attended, pullback = jax.vjp(
        core,
        linear[:, :head_size],
        linear[:, head_size : 2 * head_size],
        linear[:, 2 * head_size : 3 * head_size],
    )
    grad_query, grad_key, grad_value = pullback(grad_attn)
    small = jnp.concatenate(
        [grad_query.astype(jnp.bfloat16), grad_key.astype(jnp.bfloat16), grad_value.astype(jnp.bfloat16), attended],
        axis=1,
    )
    small_parts = [small] + [shifted(small, k) for k in range(1, count)]

    def back(small_part):
        total = None
        for i in range(3):
            term = lax.dot_general(
                small_part[:, i * head_size : (i + 1) * head_size],
                weights[i],
                (((1,), (1,)), ((), ())),
                preferred_element_type=jnp.float32,
            )
            total = term if total is None else total + term
        return total.astype(jnp.bfloat16)

    returned = [(me, back(small))]
    for k in range(1, count):
        returned.append(((me + k) % count, shifted(back(small_parts[k]), -k)))

    norm_all = jnp.concatenate(norm_parts, axis=0)
    grad_all = jnp.concatenate(grad_parts, axis=0)
    small_all = jnp.concatenate(small_parts, axis=0)
    lhs = jnp.concatenate([norm_all.T, grad_all.T], axis=0)
    summed = summed_terms(lhs, small_all, slab, head_size)

    grad_normed = jnp.zeros(tokens.shape, jnp.bfloat16)
    for place, part in returned:
        grad_normed = lax.dynamic_update_slice_in_dim(grad_normed, part, place * slab, axis=1)
    unused, norm_pull = jax.vjp(layer_norm, source)
    grad_tokens = norm_pull(grad_normed.astype(jnp.float32))[0].astype(jnp.bfloat16)
    weight_grads = summed.reshape(weights.shape).astype(jnp.float32)
    return (grad_tokens, weight_grads)


def solution(mesh):
    return jax.shard_map(
        per_device,
        mesh=mesh,
        in_specs=(
            P(("dp", "fsdp"), None),
            P(("dp", "fsdp"), None),
            P(("dp", "fsdp"), None),
            P(None, ("dp", "fsdp")),
            P(None, "fsdp", None),
        ),
        out_specs=(P(("dp", "fsdp"), None), P(None, "fsdp", None)),
        check_vma=False,
    )
```

profile of v0, /device:TPU:0, one launch (start us, length us, event | category | flops | bytes accessed | tf_op | source)
XLA Modules:
  0.0 277.2 jit_solution(17877860085245089639)
XLA Ops:
  1.6 3.0 %copy.137 = bf16[192,6144]{0,1:T(8,128)(2,1)S(1)} copy(bf16[192,6144]{1,0:T(8,128)(2,1)} %param.5) | data formatting | bytes 4718592 | tf_op args[0]
  10.0 4.5 %copy.138 = bf16[192,6144]{0,1:T(8,128)(2,1)} copy(bf16[192,6144]{1,0:T(8,128)(2,1)} %param.6) | data formatting | bytes 4718592 | tf_op args[1]
  17.3 2.8 %constant_dynamic-slice_fusion.2 = (bf16[192,3072]{0,1:T(8,128)(2,1)}, bf16[192,3072]{0,1:T(8,128)(2,1)}, bf16[192,3072]{0,1:T(8,128)(2,1)}, bf16[192,3072]{0,1:T(8,128)(2,1)}) fusion(bf16[192,6144]{0,1:T(8,128)(2,1)S(1)} %broadcast_select_fusion, s32[]{:T(128)S(6)} %select_n.47, s32[]{:T(128)S(6)} %select_n.50, bf16[192,6144]{0,1:T(8,128)(2,1)S(1)} %copy-done.3), kind=kLoop, calls=%fused_computation.164 | loop fusion | bytes 9437192 | tf_op jit(solution)/shard_map/dynamic_slice | solution.py:74
  20.1 2.6 copy.139
  22.7 3.0 %collective-permute-start = (bf16[192,3072]{1,0:T(8,128)(2,1)}, bf16[192,3072]{1,0:T(8,128)(2,1)}, u32[]{:S(2)}, u32[]{:S(2)}) collective-permute-start(bf16[192,3072]{1,0:T(8,128)(2,1)} %copy.139), channel_id=1, source_target_pairs={{0,1},{1,0},{2,3},{3,2},{4,5},{5,4},{6,7},{7,6},{8,9},{9,8},{10,11... | collective-permute-start | bytes 3538952 | tf_op jit(solution)/shard_map/ppermute | solution.py:70
  25.7 2.5 copy.140
  35.0 2.7 fusion.34
  37.7 2.7 fusion.13
  40.4 12.4 %collective-permute-done = bf16[192,3072]{1,0:T(8,128)(2,1)} collective-permute-done((bf16[192,3072]{1,0:T(8,128)(2,1)}, bf16[192,3072]{1,0:T(8,128)(2,1)}, u32[]{:S(2)}, u32[]{:S(2)}) %collective-permute-start) | collective-permute-done | bytes 1179680 | tf_op jit(solution)/shard_map/ppermute | solution.py:70
  64.5 12.7 %collective-permute-done.1 = bf16[192,3072]{1,0:T(8,128)(2,1)} collective-permute-done((bf16[192,3072]{1,0:T(8,128)(2,1)}, bf16[192,3072]{1,0:T(8,128)(2,1)}, u32[]{:S(2)}, u32[]{:S(2)}) %collective-permute-start.1) | collective-permute-done | bytes 1179680 | tf_op jit(solution)/shard_map/ppermute | solution.py:70
  82.1 2.5 copy.158
  84.6 4.2 %maximum_bitcast_fusion.1 = bf16[3072,384]{1,0:T(8,128)(2,1)} fusion(bf16[192,3072]{0,1:T(8,128)(2,1)} %copy.158, bf16[192,3072]{0,1:T(8,128)(2,1)} %get-tuple-element.20), kind=kLoop, calls=%fused_computation.23 | loop fusion | flops 4718592 | bytes 4718592 | tf_op jit(solution)/shard_map/transpose | solution.py:284
  114.4 2.7 pad_maximum_fusion.lhs_ref
  117.1 5.3 %collective-permute-done.3 = bf16[192,1024]{1,0:T(8,128)(2,1)S(1)} collective-permute-done((bf16[192,1024]{1,0:T(8,128)(2,1)S(1)}, bf16[192,1024]{1,0:T(8,128)(2,1)S(1)}, u32[]{:S(2)}, u32[]{:S(2)}) %collective-permute-start.3) | collective-permute-done | bytes 393248 | tf_op jit(solution)/shard_map/ppermute | solution.py:70
  129.5 3.4 %copy.151 = f32[192,3072]{0,1:T(8,128)} copy(f32[192,3072]{1,0:T(8,128)} %convolution_add_fusion.2) | data formatting | bytes 4718592 | tf_op jit(solution)/shard_map/add | solution.py:274
  134.9 4.8 %fusion.8 = bf16[192,6144]{0,1:T(8,128)(2,1)} fusion(bf16[192,6144]{0,1:T(8,128)(2,1)} %broadcast.258, s32[]{:T(128)S(6)} %select_n.47, f32[192,3072]{0,1:T(8,128)} %copy.151, bf16[4,3072,256]{2,1,0:T(8,128)(2,1)} %param.9, bf16[2,24,8,128]{3,2,1,0:T(8,128)(2,1)S(1)} %copy-done.14), kind=kOutput, calls=%fused_computation.16 | convolution fusion | flops 303169536 | bytes 6389764 | tf_op jit(solution)/shard_map/dot_general | solution.py:268
  139.8 107.0 %shard_map.68 = bf16[12288,256]{1,0:T(8,128)(2,1)} custom-call(bf16[6144,384]{1,0:T(8,128)(2,1)S(1)} %bitcast.160, bf16[384,1024]{1,0:T(8,128)(2,1)S(1)} %pad_maximum_fusion.1.small_ref), custom_call_target="tpu_custom_call" | custom-call | flops 1000000000 | bytes 100000000 | tf_op jit(solution)/shard_map/pallas_call | solution.py:201
  246.8 8.7 %convert.56 = f32[4,3072,256]{2,1,0:T(8,128)} convert(bf16[4,3072,256]{2,1,0:T(8,128)(2,1)} %bitcast.163) | non-fusion elementwise | flops 3145728 | bytes 18874368 | tf_op jit(solution)/shard_map/convert_element_type | solution.py:292
  255.5 2.5 copy.156
  258.0 2.7 constant_dynamic-update-slice_fusion
  260.7 3.1 %fusion.5 = f32[192]{0:T(256)S(1)} fusion(bf16[192,6144]{0,1:T(8,128)(2,1)} %constant_dynamic-update-slice_fusion, bf16[192,6144]{0,1:T(8,128)(2,1)S(1)} %copy.137, f32[192]{0:T(256)S(1)} %broadcast_multiply_fusion.2), kind=kLoop, calls=%fused_computation.10 | loop fusion | flops 5898048 | bytes 4720128 | tf_op jit(solution)/shard_map/transpose(jvp())/reduce_sum | solution.py:20
  263.8 3.6 %fusion.6 = f32[192]{0:T(256)S(1)} fusion(bf16[192,6144]{0,1:T(8,128)(2,1)S(1)} %copy.137, bf16[192,6144]{0,1:T(8,128)(2,1)} %constant_dynamic-update-slice_fusion, f32[192]{0:T(256)S(1)} %multiply_multiply_fusion.3, f32[192]{0:T(256)S(1)} %copy-done.23, f32[192]{0:T(256)S(1)} %broadcast_multiply_fusion.2), kind=kLoop, calls=%fused_computation.13 | loop fusion | flops 9436992 | bytes 4721664 | tf_op jit(solution)/shard_map/transpose(jvp())/reduce_sum | solution.py:19
  267.5 5.3 %add_convert_fusion = bf16[192,6144]{0,1:T(8,128)(2,1)} fusion(bf16[192,6144]{0,1:T(8,128)(2,1)S(1)} %copy.137, bf16[192,6144]{0,1:T(8,128)(2,1)} %constant_dynamic-update-slice_fusion, f32[192]{0:T(256)S(1)} %negate_multiply_fusion.2, f32[192]{0:T(256)S(1)} %multiply_multiply_fusion.3, f32[192]{0:T(256)S(1)} %copy-done.23, f32[192]{0:T(256)S(1)} %broadcast_multiply_fusion.2), kind=kLoop, calls=%fused_computation.11 | loop fusion | flops 10616832 | bytes 7080960 | tf_op jit(solution)/shard_map/convert_element_type | solution.py:291
  272.7 4.5 %copy.159 = bf16[192,6144]{1,0:T(8,128)(2,1)} copy(bf16[192,6144]{0,1:T(8,128)(2,1)} %add_convert_fusion) | data formatting | bytes 4718592
  (145 shorter events, 66.9 us)
Async XLA Ops:
  20.1 8.1 %copy-start.26 = (s32[2,192]{1,0:T(2,128)S(1)}, s32[2,192]{1,0:T(2,128)}, u32[]{:S(2)}) copy-start(s32[2,192]{1,0:T(2,128)} %param.8) | copy-start | bytes 4612
  22.7 30.1 %collective-permute-start = (bf16[192,3072]{1,0:T(8,128)(2,1)}, bf16[192,3072]{1,0:T(8,128)(2,1)}, u32[]{:S(2)}, u32[]{:S(2)}) collective-permute-start(bf16[192,3072]{1,0:T(8,128)(2,1)} %copy.139), channel_id=1, source_target_pairs={{0,1},{1,0},{2,3},{3,2},{4,5},{5,4},{6,7},{7,6},{8,9},{9,8},{10,11... | collective-permute-start | bytes 3538952 | tf_op jit(solution)/shard_map/ppermute | solution.py:70
  28.2 4.7 %copy-start = (bf16[192,3072]{0,1:T(8,128)(2,1)S(1)}, bf16[192,3072]{0,1:T(8,128)(2,1)}, u32[]{:S(2)}) copy-start(bf16[192,3072]{0,1:T(8,128)(2,1)} %get-tuple-element.66) | copy-start | bytes 3538948
  28.2 49.0 %collective-permute-start.1 = (bf16[192,3072]{1,0:T(8,128)(2,1)}, bf16[192,3072]{1,0:T(8,128)(2,1)}, u32[]{:S(2)}, u32[]{:S(2)}) collective-permute-start(bf16[192,3072]{1,0:T(8,128)(2,1)} %copy.140), channel_id=1, source_target_pairs={{0,1},{1,0},{2,3},{3,2},{4,5},{5,4},{6,7},{7,6},{8,9},{9,8},{10,11... | collective-permute-start | bytes 3538952 | tf_op jit(solution)/shard_map/ppermute | solution.py:70
  32.9 4.8 %copy-start.2 = (bf16[192,3072]{0,1:T(8,128)(2,1)S(1)}, bf16[192,3072]{0,1:T(8,128)(2,1)}, u32[]{:S(2)}) copy-start(bf16[192,3072]{0,1:T(8,128)(2,1)} %get-tuple-element.20) | copy-start | bytes 3538948
  57.5 4.7 %copy-start.1 = (bf16[192,3072]{0,1:T(8,128)(2,1)S(1)}, bf16[192,3072]{0,1:T(8,128)(2,1)}, u32[]{:S(2)}) copy-start(bf16[192,3072]{0,1:T(8,128)(2,1)} %get-tuple-element.66) | copy-start | bytes 3538948
  57.6 4.7 %copy-start.6 = (bf16[192,3072]{0,1:T(8,128)(2,1)S(1)}, bf16[192,3072]{0,1:T(8,128)(2,1)}, u32[]{:S(2)}) copy-start(bf16[192,3072]{0,1:T(8,128)(2,1)} %copy.157) | copy-start | bytes 3538948
  80.3 10.6 %collective-permute-start.2 = (bf16[192,1024]{1,0:T(8,128)(2,1)}, bf16[192,1024]{1,0:T(8,128)(2,1)}, u32[]{:S(2)}, u32[]{:S(2)}) collective-permute-start(bf16[192,1024]{1,0:T(8,128)(2,1)} %pad_maximum_fusion.2), channel_id=1, source_target_pairs={{0,1},{1,0},{2,3},{3,2},{4,5},{5,4},{6,7},{7,6},{8,9},{9,8},{10,11... | collective-permute-start | bytes 1179656 | tf_op jit(solution)/shard_map/ppermute | solution.py:70
  84.6 6.4 %copy-start.15 = (f32[192,256]{1,0:T(8,128)S(1)}, f32[192,256]{1,0:T(8,128)}, u32[]{:S(2)}) copy-start(f32[192,256]{1,0:T(8,128)} %fusion.34) | copy-start | bytes 589828
  84.6 6.4 %copy-start.16 = (f32[192,256]{1,0:T(8,128)S(1)}, f32[192,256]{1,0:T(8,128)}, u32[]{:S(2)}) copy-start(f32[192,256]{1,0:T(8,128)} %fusion.13) | copy-start | bytes 589828
  104.4 4.2 %copy-start.21 = (pred[192,192]{0,1:T(8,128)(4,1)S(1)}, pred[192,192]{0,1:T(8,128)(4,1)}, u32[]{:S(2)}) copy-start(pred[192,192]{0,1:T(8,128)(4,1)} %broadcast_compare_fusion) | copy-start | bytes 110596
  104.4 4.5 %copy-start.19 = (bf16[24,2,8,128]{3,2,1,0:T(8,128)(2,1)S(1)}, bf16[24,2,8,128]{3,2,1,0:T(8,128)(2,1)}, u32[]{:S(2)}) copy-start(bf16[24,2,8,128]{3,2,1,0:T(8,128)(2,1)} %get-tuple-element.37) | copy-start | bytes 294916
  104.4 4.5 %copy-start.20 = (bf16[24,2,8,128]{3,2,1,0:T(8,128)(2,1)S(1)}, bf16[24,2,8,128]{3,2,1,0:T(8,128)(2,1)}, u32[]{:S(2)}) copy-start(bf16[24,2,8,128]{3,2,1,0:T(8,128)(2,1)} %get-tuple-element.36) | copy-start | bytes 294916
  110.3 4.1 %copy-start.4 = (bf16[3072,384]{1,0:T(8,128)(2,1)S(1)}, bf16[3072,384]{1,0:T(8,128)(2,1)}, u32[]{:S(2)}) copy-start(bf16[3072,384]{1,0:T(8,128)(2,1)} %maximum_bitcast_fusion) | copy-start | bytes 7077892
  111.1 11.3 %slice-start.2 = ((s8[6291456]{0:T(1024)(128)(4,1)}), s8[4194304]{0:T(1024)(128)(4,1)S(1)}, s32[]{:S(2)}) async-start(s8[6291456]{0:T(1024)(128)(4,1)} %bitcast.161), calls=%async_computation.2 | async-start | bytes 8388608
  112.9 4.2 %copy-start.17 = (bf16[192,1024]{1,0:T(8,128)(2,1)}, bf16[192,1024]{1,0:T(8,128)(2,1)S(1)}, u32[]{:S(2)}) copy-start(bf16[192,1024]{1,0:T(8,128)(2,1)S(1)} %bitcast_dynamic-update-slice_fusion) | copy-start | bytes 1179652
  112.9 9.5 %slice-start.3 = ((s8[6291456]{0:T(1024)(128)(4,1)}), s8[2097152]{0:T(1024)(128)(4,1)S(1)}, s32[]{:S(2)}) async-start(s8[6291456]{0:T(1024)(128)(4,1)} %bitcast.161), calls=%async_computation.3 | async-start | bytes 4194304
  112.9 9.4 %collective-permute-start.3 = (bf16[192,1024]{1,0:T(8,128)(2,1)S(1)}, bf16[192,1024]{1,0:T(8,128)(2,1)S(1)}, u32[]{:S(2)}, u32[]{:S(2)}) collective-permute-start(bf16[192,1024]{1,0:T(8,128)(2,1)S(1)} %bitcast_dynamic-update-slice_fusion), channel_id=1, source_target_pairs={{0,1},{1,0},{2,3},{3,2},{4,5},{5,4},{6,7},{7,6},{8,9},{9,8},{10,11... | collective-permute-start | bytes 1179656 | tf_op jit(solution)/shard_map/ppermute | solution.py:70
  125.4 130.1 %collective-permute-start.4 = (bf16[192,3072]{1,0:T(8,128)(2,1)}, bf16[192,3072]{1,0:T(8,128)(2,1)}, u32[]{:S(2)}, u32[]{:S(2)}) collective-permute-start(bf16[192,3072]{1,0:T(8,128)(2,1)} %fusion.10), channel_id=1, source_target_pairs={{0,1},{1,0},{2,3},{3,2},{4,5},{5,4},{6,7},{7,6},{8,9},{9,8},{10,11... | collective-permute-start | bytes 3538952 | tf_op jit(solution)/shard_map/ppermute | solution.py:70
  129.5 5.3 %copy-start.14 = (bf16[2,24,8,128]{3,2,1,0:T(8,128)(2,1)S(1)}, bf16[2,24,8,128]{3,2,1,0:T(8,128)(2,1)}, u32[]{:S(2)}) copy-start(bf16[2,24,8,128]{3,2,1,0:T(8,128)(2,1)} %copy-done.13) | copy-start | bytes 294916
  133.0 6.8 %slice-start = ((s8[4718592]{0:T(1024)(128)(4,1)}), s8[4194304]{0:T(1024)(128)(4,1)S(1)}, s32[]{:S(2)}) async-start(s8[4718592]{0:T(1024)(128)(4,1)} %bitcast.159), calls=%async_computation | async-start | bytes 8388608
  134.9 4.8 %copy-start.12 = (bf16[192,1024]{1,0:T(8,128)(2,1)S(1)}, bf16[192,1024]{1,0:T(8,128)(2,1)}, u32[]{:S(2)}) copy-start(bf16[192,1024]{1,0:T(8,128)(2,1)} %copy-done.11) | copy-start | bytes 1179652
  134.9 4.8 %copy-start.18 = (bf16[192,1024]{1,0:T(8,128)(2,1)S(1)}, bf16[192,1024]{1,0:T(8,128)(2,1)}, u32[]{:S(2)}) copy-start(bf16[192,1024]{1,0:T(8,128)(2,1)} %copy-done.17) | copy-start | bytes 1179652
  134.9 4.9 %slice-start.1 = ((s8[4718592]{0:T(1024)(128)(4,1)}), s8[524288]{0:T(1024)(128)(4,1)S(1)}, s32[]{:S(2)}) async-start(s8[4718592]{0:T(1024)(128)(4,1)} %bitcast.159), calls=%async_computation.1 | async-start | bytes 1048576
  (12 other events, 23.8 us)
where the time goes:
time: 279 us; the launch traced here: 277 us
  Pallas kernels  107 us (38%)
  other arithmetic  53.1 us (19%)
  local copies, waits for them, and re-layouts  44.8 us (16%)
  waiting for transfers between devices  32.5 us (12%)
  matrix products  31.4 us (11%)
  starting transfers between devices  7.31 us (3%)
    pallas_call x1, Pallas kernels, summed_terms(): pl.pallas_call(functools.partial(sum_kernel, orders, slab, head_size), ou...  107 us
    ppermute x5, waiting for transfers between devices, shifted(): lax.ppermute(value, 'fsdp', [(i, (i + offset) % count) for i in range(cou...  32.5 us
    unnamed x67, local copies, waits for them, and re-layouts  14.5 us
    dot_general x6, matrix products, products(): jnp.dot(norm_part, weights[i], preferred_element_type=jnp.float32)  14.2 us
    dot_general x6, matrix products, back(): lax.dot_general(small_part[:, i * head_size:(i + 1) * head_size], weights...  10.8 us
    reduce_sum x6, other arithmetic, layer_norm(): center = values - jnp.mean(values, axis=-1, keepdims=True)  8.88 us
    convert_element_type x1, other arithmetic, per_device(): weight_grads = summed.reshape(weights.shape).astype(jnp.float32)  8.67 us
    dynamic_slice x3, local copies, waits for them, and re-layouts, part_of(): return lax.dynamic_slice_in_dim(values, index * width, width, axis=1)  7.92 us
  transfers between devices with their start and end apart: 5, of which 4 were waited for; matrix products, arithmetic and copies ran while one was open for 21% of the time, Pallas kernels for 39%

commit v1 on v0

v1 whole, which is shorter than its diff:
```python
import functools
import math

import jax
import jax.numpy as jnp
from jax import lax
from jax.experimental import pallas as pl
from jax.experimental.pallas import tpu as pltpu
from jax.sharding import PartitionSpec as P

HD = 128
TILE = 256

EPS = 1e-06
rope_base = 100.0


def side_tables(lengths, positions, capacity):
    ends = [lengths[0, 0], lengths[0, 0] + lengths[0, 1], lengths[0, 0] + lengths[0, 1] + lengths[0, 2]]

    def slots(rows):
        slot = sum((rows >= end).astype(jnp.float32) for end in ends)
        return jnp.where(slot < 3, slot, -1.0)

    column = slots(lax.broadcasted_iota(jnp.int32, (capacity, 1), 0))
    line = slots(lax.broadcasted_iota(jnp.int32, (8, capacity), 1))
    lane = lax.broadcasted_iota(jnp.int32, (capacity, HD), 1)
    quarter = HD // 4
    frequency = rope_base ** (-(lane % quarter).astype(jnp.float32) / quarter)
    place = jnp.where(lane < HD // 2, positions[0][:, None], positions[1][:, None]).astype(jnp.float32)
    angles = place * frequency
    sign = jnp.where((lane // quarter) % 2 == 0, -1.0, 1.0)
    return column, line, jnp.cos(angles), sign * jnp.sin(angles)


def normalize(values):
    center = values - jnp.mean(values, axis=-1, keepdims=True)
    scale = lax.rsqrt(jnp.mean(center * center, axis=-1, keepdims=True) + EPS)
    return center * scale, scale


def normalize_back(grad, normal, scale):
    inner = jnp.mean(grad * normal, axis=-1, keepdims=True)
    return scale * (grad - jnp.mean(grad, axis=-1, keepdims=True) - normal * inner)


def swap_quarters(values):
    quarter = HD // 4
    lane = lax.broadcasted_iota(jnp.int32, values.shape, 1)
    return jnp.where(
        (lane // quarter) % 2 == 0, pltpu.roll(values, HD - quarter, 1), pltpu.roll(values, quarter, 1)
    )


def dot(left, right):
    return jnp.dot(left, right, preferred_element_type=jnp.float32)


def dot_nt(left, right):
    return lax.dot_general(left, right, (((1,), (1,)), ((), ())), preferred_element_type=jnp.float32)


def layer_kernel(
    orders, tokens_ref, cot_ref, column_ref, line_ref, cos_ref, sin_ref, weights_hbm, out_ref, tokens_out,
    weights, normed, gout, norm_in, gout_in, mean_ref, scale_ref, linear, lin_send, lin_in, attn_send, attn_in,
    lhs_ref, small, back, back_send, acc, outgoing, incoming, w_sem, y_send, y_recv, send_sem, recv_sem,
):
    capacity = tokens_ref.shape[0]
    slab, head_size = weights.shape[1], weights.shape[2]
    shards = normed.shape[0]
    heads = head_size // HD
    me = lax.axis_index("dp")
    shard = lax.axis_index("fsdp")
    streams, steps = len(orders), len(orders[0])
    rows = 4 * slab // streams
    halves = [rows >> (s + 1) for s in range(steps)]
    starts = [rows - 2 * halves[s] for s in range(steps)]
    bit_of = [(me // (1 << bit)) % 2 for bit in range(steps)]
    peer_of = [me + (1 - 2 * bit_of[bit]) * (1 << bit) for bit in range(steps)]
    others = range(1, shards)

    fetch = pltpu.make_async_copy(weights_hbm, weights, w_sem)
    fetch.start()
    barrier = pltpu.get_barrier_semaphore()
    for bit in range(steps):
        pl.semaphore_signal(barrier, inc=1, device_id={"dp": peer_of[bit]}, device_id_type=pl.DeviceIdType.MESH)
    for k in others:
        pl.semaphore_signal(
            barrier, inc=1, device_id={"fsdp": (shard + k) % shards}, device_id_type=pl.DeviceIdType.MESH
        )

    started = []

    def across(kind, k, direction, source, target):
        copy = pltpu.make_async_remote_copy(
            src_ref=source,
            dst_ref=target,
            send_sem=y_send.at[kind, k],
            recv_sem=y_recv.at[kind, k],
            device_id={"fsdp": (shard + shards + direction * k) % shards},
            device_id_type=pl.DeviceIdType.MESH,
        )
        copy.start()
        started.append(copy)
        return copy

    chunk = capacity // 2
    parts = [pl.ds(0, chunk), pl.ds(chunk, chunk)]
    group = 16

    def mask_cotangent(part):
        @pl.loop(0, chunk // group)
        def masked(t):
            at = pl.ds(pl.multiple_of(part * chunk + t * group, group), group)
            live = (column_ref[at, :] >= 0).astype(jnp.float32)
            for p in range(shards):
                value = cot_ref[at, p * slab : (p + 1) * slab].astype(jnp.float32)
                gout[p, at, :] = (value * live).astype(jnp.bfloat16)

    def normalize_tokens(part):
        @pl.loop(0, chunk // group)
        def normal(t):
            at = pl.ds(pl.multiple_of(part * chunk + t * group, group), group)
            value = tokens_ref[at, :].astype(jnp.float32)
            mean = jnp.mean(value, axis=-1, keepdims=True)
            center = value - mean
            scale = lax.rsqrt(jnp.mean(center * center, axis=-1, keepdims=True) + EPS)
            mean_ref[at, :] = jnp.broadcast_to(mean, (group, HD))
            scale_ref[at, :] = jnp.broadcast_to(scale, (group, HD))
            result = (center * scale).astype(jnp.bfloat16)
            for p in range(shards):
                normed[p, at, :] = result[:, p * slab : (p + 1) * slab]

    gout_copies, norm_copies = {}, {}

    def send_gout(part):
        for k in others:
            gout_copies[part, k] = across(
                part, k, 1, gout.at[(shard + k) % shards, parts[part]], gout_in.at[k - 1, parts[part]]
            )

    def send_norm(part):
        for k in others:
            norm_copies[part, k] = across(
                2 + part, k, 1, normed.at[(shard + k) % shards, parts[part]], norm_in.at[k - 1, parts[part]]
            )

    mask_cotangent(0)
    pl.semaphore_wait(barrier, steps + shards - 1)
    send_gout(0)
    normalize_tokens(0)
    send_norm(0)
    normalize_tokens(1)
    send_norm(1)
    mask_cotangent(1)
    send_gout(1)

    fetch.wait()
    for i in range(3):
        linear[:, i * head_size : (i + 1) * head_size] = dot(normed[shard], weights[i])
    linear[:, 3 * head_size :] = dot(gout[shard], weights[3])

    lin_copies, attn_copies = {}, {}

    def attn_partial(part):
        for k in others:
            gout_copies[part, k].wait_recv()
            attn_send[k - 1, parts[part], :] = dot(gout_in[k - 1, parts[part], :], weights[3]).astype(jnp.bfloat16)
            attn_copies[part, k] = across(
                4 + part, k, -1, attn_send.at[k - 1, parts[part]], attn_in.at[k - 1, parts[part]]
            )

    def lin_partial(part):
        for k in others:
            norm_copies[part, k].wait_recv()
            for i in range(3):
                lin_send[k - 1, parts[part], i * head_size : (i + 1) * head_size] = dot(
                    norm_in[k - 1, parts[part], :], weights[i]
                ).astype(jnp.bfloat16)
            lin_copies[part, k] = across(
                6 + part, k, -1, lin_send.at[k - 1, parts[part]], lin_in.at[k - 1, parts[part]]
            )

    attn_partial(0)
    lin_partial(0)
    lin_partial(1)

    def transpose_into(base, own, arrived):
        @pl.loop(0, slab // TILE)
        def turn(t):
            at = pl.ds(pl.multiple_of(t * TILE, TILE), TILE)
            whole = jnp.concatenate([own[shard, :, at]] + [arrived[k - 1, :, at] for k in others], axis=0)
            lhs_ref[pl.ds(pl.multiple_of(base + t * TILE, TILE), TILE), :] = whole.T

    transpose_into(0, normed, norm_in)
    for part in range(2):
        for k in others:
            lin_copies[part, k].wait_recv()
            linear[parts[part], : 3 * head_size] += lin_in[k - 1, parts[part], :].astype(jnp.float32)

    cosine, sine = cos_ref[...], sin_ref[...]
    same = column_ref[...] == line_ref[0:1, :]
    score_scale = 1.0 / math.sqrt(HD)
    saved = []
    for h in range(heads):
        normals = []
        turned = []
        for which in range(2):
            first = which * head_size + h * HD
            normal, scale = normalize(linear[:, first : first + HD])
            normals.append((normal, scale))
            turned.append((normal * cosine + swap_quarters(normal) * sine).astype(jnp.bfloat16))
        first = 2 * head_size + h * HD
        values = linear[:, first : first + HD].astype(jnp.bfloat16)
        queries, keys = turned
        exponent = jnp.where(same, jnp.exp(dot_nt(queries, keys) * score_scale), 0.0)
        prob = exponent / jnp.sum(exponent, axis=1, keepdims=True)
        exponent = jnp.where(same, jnp.exp(dot_nt(keys, queries) * score_scale), 0.0)
        prob_t = exponent / jnp.sum(exponent, axis=0, keepdims=True)
        small[3, 0:capacity, h * HD : (h + 1) * HD] = dot(prob.astype(jnp.bfloat16), values).astype(jnp.bfloat16)
        saved.append((normals, queries, keys, values, prob, prob_t))
    arrivals = [
        across(8, k, 1, small.at[3, pl.ds(0, capacity)], small.at[3, pl.ds(k * capacity, capacity)]) for k in others
    ]

    attn_partial(1)
    transpose_into(slab, gout, gout_in)
    for part in range(2):
        for k in others:
            attn_copies[part, k].wait_recv()
            linear[parts[part], 3 * head_size :] += attn_in[k - 1, parts[part], :].astype(jnp.float32)

    for h in range(heads):
        normals, queries, keys, values, prob, prob_t = saved[h]
        first = 3 * head_size + h * HD
        grad = linear[:, first : first + HD].astype(jnp.bfloat16)
        grad_prob = dot_nt(grad, values).astype(jnp.bfloat16).astype(jnp.float32)
        grad_score = prob * (grad_prob - jnp.sum(grad_prob * prob, axis=1, keepdims=True)) * score_scale
        grad_prob = dot_nt(values, grad).astype(jnp.bfloat16).astype(jnp.float32)
        grad_score_t = prob_t * (grad_prob - jnp.sum(grad_prob * prob_t, axis=0, keepdims=True)) * score_scale
        gradients = [
            dot(grad_score.astype(jnp.bfloat16), keys),
            dot(grad_score_t.astype(jnp.bfloat16), queries),
        ]
        place = slice(h * HD, (h + 1) * HD)
        for which in range(2):
            gradient = gradients[which].astype(jnp.bfloat16).astype(jnp.float32)
            gradient = gradient * cosine + swap_quarters(gradient * sine)
            small[which, 0:capacity, place] = normalize_back(gradient, *normals[which]).astype(jnp.bfloat16)
        small[2, 0:capacity, place] = dot(prob_t.astype(jnp.bfloat16), grad).astype(jnp.bfloat16)
    arrivals += [
        across(
            9, k, 1, small.at[pl.ds(0, 3), pl.ds(0, capacity)], small.at[pl.ds(0, 3), pl.ds(k * capacity, capacity)]
        )
        for k in others
    ]

    def slice_gradient(slot, store):
        @pl.loop(0, slab // TILE)
        def tile(t):
            at = pl.ds(pl.multiple_of(t * TILE, TILE), TILE)
            total = sum(
                dot_nt(small[i, slot * capacity : (slot + 1) * capacity, :], weights[i, at, :]) for i in range(3)
            )
            store(at, total.astype(jnp.bfloat16))

    def own_slice(at, value):
        back[shard, :, at] = value

    slice_gradient(0, own_slice)
    for copy in arrivals:
        copy.wait_recv()

    back_copies = []

    def return_gradients():
        for k in others:

            def keep(at, value):
                back_send[k - 1, :, at] = value

            slice_gradient(k, keep)
            back_copies.append(across(10, k, -1, back_send.at[k - 1], back.at[shard]))

    def token_gradients():
        for copy in back_copies:
            copy.wait_recv()

        @pl.loop(0, capacity // group)
        def piece(t):
            at = pl.ds(pl.multiple_of(t * group, group), group)
            scale = scale_ref[at, 0:1]
            normal = (tokens_ref[at, :].astype(jnp.float32) - mean_ref[at, 0:1]) * scale
            grad = jnp.concatenate([back[p, at, :] for p in range(shards)], axis=1).astype(jnp.float32)
            tokens_out[at, :] = normalize_back(grad, normal, scale).astype(jnp.bfloat16)

    def term(stream, row):
        row = stream * rows + row
        weight = row // slab
        left = pl.multiple_of((weight // 3) * slab + row % slab, TILE)
        return dot(lhs_ref[pl.ds(left, TILE), :], small[weight])

    def exchange(phase, stream, step, source, target):
        copy = pltpu.make_async_remote_copy(
            src_ref=source,
            dst_ref=target,
            send_sem=send_sem.at[phase, stream, step],
            recv_sem=recv_sem.at[phase, stream, step],
            device_id={"dp": peer_of[orders[stream][step]]},
            device_id_type=pl.DeviceIdType.MESH,
        )
        copy.start()
        return copy

    copies = {}
    offsets = {}
    for stream in range(streams):
        half = halves[0]
        mine = bit_of[orders[stream][0]]

        @pl.loop(0, half // TILE)
        def leaving(t):
            value = term(stream, (1 - mine) * half + t * TILE)
            outgoing[stream, pl.ds(pl.multiple_of(t * TILE, TILE), TILE), :] = value.astype(jnp.bfloat16)

        copies[0, stream, 0] = exchange(
            0, stream, 0, outgoing.at[stream, pl.ds(0, half)], incoming.at[stream, pl.ds(0, half)]
        )
        offsets[stream, 0] = mine * half

    for stream in range(streams):
        half = halves[0]
        mine = bit_of[orders[stream][0]]

        @pl.loop(0, half // TILE)
        def kept(t):
            acc[stream, pl.ds(pl.multiple_of(t * TILE, TILE), TILE), :] = term(stream, mine * half + t * TILE)

    return_gradients()

    for step in range(1, steps + 1):
        for stream in range(streams):
            copies[0, stream, step - 1].wait_recv()
            got = starts[step - 1]
            base = offsets[stream, step - 1] - offsets[stream, 0]
            if step < steps:
                half = halves[step]
                size = min(half, 192)
                mine = bit_of[orders[stream][step]]
                go, stay = (1 - mine) * half, mine * half

                @pl.loop(0, half // size)
                def leaving(t):
                    at = pl.multiple_of(t * size, size)
                    value = acc[stream, pl.ds(pl.multiple_of(base + go + at, size), size), :]
                    other = incoming[stream, pl.ds(pl.multiple_of(got + go + at, size), size), :]
                    outgoing[stream, pl.ds(pl.multiple_of(starts[step] + at, size), size), :] = (
                        value + other.astype(jnp.float32)
                    ).astype(jnp.bfloat16)

                place = pl.ds(starts[step], half)
                copies[0, stream, step] = exchange(
                    0, stream, step, outgoing.at[stream, place], incoming.at[stream, place]
                )

                @pl.loop(0, half // size)
                def kept(t):
                    at = pl.multiple_of(t * size, size)
                    where = pl.ds(pl.multiple_of(base + stay + at, size), size)
                    other = incoming[stream, pl.ds(pl.multiple_of(got + stay + at, size), size), :]
                    acc[stream, where, :] = acc[stream, where, :] + other.astype(jnp.float32)

                offsets[stream, step] = offsets[stream, step - 1] + stay
            else:
                half = halves[steps - 1]
                place = pl.ds(pl.multiple_of(stream * rows + offsets[stream, steps - 1], half), half)
                value = acc[stream, pl.ds(pl.multiple_of(base, half), half), :]
                other = incoming[stream, pl.ds(got, half), :]
                out_ref[place, :] = (value + other.astype(jnp.float32)).astype(jnp.bfloat16)
                copies[1, stream, steps - 1] = exchange(
                    1, stream, steps - 1, out_ref.at[place], out_ref.at[place]
                )

    token_gradients()

    for step in reversed(range(steps - 1)):
        for stream in range(streams):
            copies[1, stream, step + 1].wait_recv()
            half = halves[step]
            place = pl.ds(pl.multiple_of(stream * rows + offsets[stream, step], half), half)
            copies[1, stream, step] = exchange(1, stream, step, out_ref.at[place], out_ref.at[place])
    for stream in range(streams):
        copies[1, stream, 0].wait_recv()
    for copy in copies.values():
        copy.wait_send()
    for copy in started:
        copy.wait_send()


def per_device(tokens, cotangent, lengths, positions, weights):
    capacity, width = tokens.shape
    slab, head_size = weights.shape[1:]
    shards = lax.axis_size("fsdp")
    steps = lax.axis_size("dp").bit_length() - 1
    streams = 4 if (slab >> steps) % 16 == 0 else 2
    rows = 4 * slab // streams
    plain = list(range(steps))
    turned = plain[:1] + plain[2:] + plain[1:2]
    orders = [turned] + [plain] * (streams - 1)
    moved = rows - (rows >> steps)
    column, line, cosine, sine = side_tables(lengths, positions, capacity)
    vmem = pl.BlockSpec(memory_space=pltpu.VMEM)
    half = jnp.bfloat16
    summed, grad_tokens = pl.pallas_call(
        functools.partial(layer_kernel, orders),
        out_shape=(
            jax.ShapeDtypeStruct((4 * slab, head_size), half),
            jax.ShapeDtypeStruct((capacity, width), half),
        ),
        in_specs=[vmem] * 6 + [pl.BlockSpec(memory_space=pl.ANY)],
        out_specs=(vmem, vmem),
        scratch_shapes=[
            pltpu.VMEM((4, slab, head_size), half),
            pltpu.VMEM((shards, capacity, slab), half),
            pltpu.VMEM((shards, capacity, slab), half),
            pltpu.VMEM((shards - 1, capacity, slab), half),
            pltpu.VMEM((shards - 1, capacity, slab), half),
            pltpu.VMEM((capacity, HD), jnp.float32),
            pltpu.VMEM((capacity, HD), jnp.float32),
            pltpu.VMEM((capacity, 4 * head_size), jnp.float32),
            pltpu.VMEM((shards - 1, capacity, 3 * head_size), half),
            pltpu.VMEM((shards - 1, capacity, 3 * head_size), half),
            pltpu.VMEM((shards - 1, capacity, head_size), half),
            pltpu.VMEM((shards - 1, capacity, head_size), half),
            pltpu.VMEM((2 * slab, shards * capacity), half),
            pltpu.VMEM((4, shards * capacity, head_size), half),
            pltpu.VMEM((shards, capacity, slab), half),
            pltpu.VMEM((shards - 1, capacity, slab), half),
            pltpu.VMEM((streams, rows // 2, head_size), jnp.float32),
            pltpu.VMEM((streams, moved, head_size), half),
            pltpu.VMEM((streams, moved, head_size), half),
            pltpu.SemaphoreType.DMA,
            pltpu.SemaphoreType.DMA((11, shards)),
            pltpu.SemaphoreType.DMA((11, shards)),
            pltpu.SemaphoreType.DMA((2, streams, steps)),
            pltpu.SemaphoreType.DMA((2, streams, steps)),
        ],
        compiler_params=pltpu.CompilerParams(
            collective_id=0, has_side_effects=True, vmem_limit_bytes=62 * 1024 * 1024
        ),
        cost_estimate=pl.CostEstimate(flops=4 * 10**9, bytes_accessed=10**8, transcendentals=10**5),
    )(tokens, cotangent, column, line, cosine, sine, weights)
    return (grad_tokens, summed.reshape(weights.shape).astype(jnp.float32))


def solution(mesh):
    return jax.shard_map(
        per_device,
        mesh=mesh,
        in_specs=(
            P(("dp", "fsdp"), None),
            P(("dp", "fsdp"), None),
            P(("dp", "fsdp"), None),
            P(None, ("dp", "fsdp")),
            P(None, "fsdp", None),
        ),
        out_specs=(P(("dp", "fsdp"), None), P(None, "fsdp", None)),
        check_vma=False,
    )
```

time: 279 us -> 205 us (0.73)
  Pallas kernels: 107 us -> 186 us
  local copies, waits for them, and re-layouts: 44.8 us -> 3.59 us
  other arithmetic: 53.1 us -> 12.6 us
  waiting for transfers between devices: 32.5 us -> 0 us
  matrix products: 31.4 us -> 0 us
  starting transfers between devices: 7.31 us -> 0 us
    pallas_call x1, Pallas kernels: 107 us -> 186 us  [per_device(): pl.pallas_call(functools.partial(layer_kernel, orders), out_shape=(jax.Sh...]
    ppermute x5 -> x0, waiting for transfers between devices: 32.5 us -> none  [shifted(): lax.ppermute(value, 'fsdp', [(i, (i + offset) % count) for i in range(cou...]
    dot_general x20 -> x0, matrix products: 31.4 us -> none  [the longest x6 14.2 us: products(): jnp.dot(norm_part, weights[i], preferred_element_type=jnp.float32)]
    reduce_sum x13 -> x0, other arithmetic: 14.4 us -> none  [the longest x6 8.88 us: layer_norm(): center = values - jnp.mean(values, axis=-1, keepdims=True)]
    unnamed x67 -> x3, local copies, waits for them, and re-layouts: 14.5 us -> 1.41 us
    dynamic_slice x3 -> x0, local copies, waits for them, and re-layouts: 7.92 us -> none  [part_of(): return lax.dynamic_slice_in_dim(values, index * width, width, axis=1)]
    convert_element_type x4 -> x1, other arithmetic: 16.4 us -> 8.82 us  [per_device(): return (grad_tokens, summed.reshape(weights.shape).astype(jnp.float32))]
    ppermute x3 -> x0, local copies, waits for them, and re-layouts: 7.52 us -> none  [shifted(): lax.ppermute(value, 'fsdp', [(i, (i + offset) % count) for i in range(cou...]
  transfers between devices with their start and end apart: 5 -> 0, of which waited for: 4 -> 0; matrix products, arithmetic and copies ran while one was open for 21% -> 0% of each run, Pallas kernels for 39% -> 0%
where the time goes in v1:
time: 205 us
  Pallas kernels  186 us (91%)
  other arithmetic  12.6 us (6%)
  local copies, waits for them, and re-layouts  3.59 us (2%)
  between operations  2.66 us (1%)
    pallas_call x1, Pallas kernels, per_device(): pl.pallas_call(functools.partial(layer_kernel, orders), out_shape=(jax.Sh...  186 us
    convert_element_type x1, other arithmetic, per_device(): return (grad_tokens, summed.reshape(weights.shape).astype(jnp.float32))  8.82 us

profile of v1, /device:TPU:0, one launch (start us, length us, event | category | flops | bytes accessed | tf_op | source)
XLA Modules:
  0.0 204.6 jit_solution(8756201825976167384)
XLA Ops:
  0.7 1.4 fusion.7
  4.1 0.7 broadcast_compare_fusion
  4.7 0.8 fusion.6
  5.5 0.6 broadcast_select_fusion.line_ref
  6.1 1.3 compare_select_fusion.column_ref
  7.4 1.2 sine_multiply_fusion
  8.6 185.8 %shard_map.68 = (bf16[12288,256]{1,0:T(8,128)(2,1)}, bf16[192,6144]{1,0:T(8,128)(2,1)}) custom-call(bf16[192,6144]{1,0:T(8,128)(2,1)} %tokens_ref.1, bf16[192,6144]{1,0:T(8,128)(2,1)} %cot_ref.1, f32[192,1]{1,0:T(8,128)} %compare_select_fusion.column_ref, f32[8,192]{1,0:T(8,128)} %broadcast_select_fusion.line_ref, f32[192,128]{1,0:T(8,128)} %get-tuple-element.9.cos_ref, ...), custom_call_target="tpu_custom_call" | custom-call | flops 4000000000 | bytes 100000000 | tf_op jit(solution)/shard_map/pallas_call | solution.py:414
  194.3 0.0 copy-start
  194.4 8.8 %convert.1 = f32[4,3072,256]{2,1,0:T(8,128)} convert(bf16[4,3072,256]{2,1,0:T(8,128)(2,1)} %bitcast.7) | non-fusion elementwise | flops 3145728 | bytes 18874368 | tf_op jit(solution)/shard_map/convert_element_type | solution.py:453
  203.2 0.0 copy-done
  203.2 1.4 copy.8
  (4 shorter events, 0.0 us)
Async XLA Ops:
  194.3 8.8 %copy-start = (bf16[192,6144]{1,0:T(8,128)(2,1)S(1)}, bf16[192,6144]{1,0:T(8,128)(2,1)}, u32[]{:S(2)}) copy-start(bf16[192,6144]{1,0:T(8,128)(2,1)} %get-tuple-element.23) | copy-start | bytes 7077892

commit v2 on v1

--- a/solution.py
+++ b/solution.py
@@ -15,22 +15,70 @@
 rope_base = 100.0
 
 
-def side_tables(lengths, positions, capacity):
-    ends = [lengths[0, 0], lengths[0, 0] + lengths[0, 1], lengths[0, 0] + lengths[0, 1] + lengths[0, 2]]
-
-    def slots(rows):
-        slot = sum((rows >= end).astype(jnp.float32) for end in ends)
-        return jnp.where(slot < 3, slot, -1.0)
-
-    column = slots(lax.broadcasted_iota(jnp.int32, (capacity, 1), 0))
-    line = slots(lax.broadcasted_iota(jnp.int32, (8, capacity), 1))
+def segment_slots(lengths_ref, rows):
+    end = 0
+    slot = jnp.zeros(rows.shape, jnp.float32)
+    for image in range(3):
+        end = end + lengths_ref[0, image]
+        slot = slot + jnp.where(rows >= end, 1.0, 0.0)
+    return jnp.where(slot < 3.0, slot, -1.0)
+
+
+def rotary_tables(positions_ref):
+    capacity = positions_ref.shape[1]
+    down = lax.broadcasted_iota(jnp.int32, (capacity, capacity), 0)
+    along = lax.broadcasted_iota(jnp.int32, (capacity, capacity), 1)
+
+    def column(i):
+        line = positions_ref[i : i + 1, :].astype(jnp.float32)
+        return jnp.sum(jnp.where(down == along, line, 0.0), axis=1, keepdims=True)
+
     lane = lax.broadcasted_iota(jnp.int32, (capacity, HD), 1)
     quarter = HD // 4
-    frequency = rope_base ** (-(lane % quarter).astype(jnp.float32) / quarter)
-    place = jnp.where(lane < HD // 2, positions[0][:, None], positions[1][:, None]).astype(jnp.float32)
-    angles = place * frequency
+    frequency = jnp.exp((lane % quarter).astype(jnp.float32) * (-math.log(rope_base) / quarter))
+    angles = jnp.where(lane < HD // 2, column(0), column(1)) * frequency
     sign = jnp.where((lane // quarter) % 2 == 0, -1.0, 1.0)
-    return column, line, jnp.cos(angles), sign * jnp.sin(angles)
+    return jnp.cos(angles), sign * jnp.sin(angles)
+
+
+def exchange_plan(orders, halves):
+    streams, steps = len(orders), len(halves)
+    stages = [(0, s) for s in range(steps)] + [(1, s) for s in reversed(range(steps))]
+    link = lambda bit: min(bit, 2)
+    busy = {0: 0.0, 1: 0.0, 2: 0.0}
+    flying = {0: 0, 1: 0, 2: 0}
+    waiting = {0: [], 1: [], 2: []}
+    depth = {0: streams, 1: 2, 2: 2}
+    events, plan = [], []
+
+    def launch(now, stream, place):
+        step = stages[place][1]
+        bit = orders[stream][step]
+        kind = link(bit)
+        if flying[kind] >= depth[kind]:
+            waiting[kind].append((stream, place))
+            return
+        flying[kind] += 1
+        cost = halves[step] * 0.0114 * (0.2 if bit == 0 else 1.0 if bit < 3 else 1.4)
+        busy[kind] = max(busy[kind], now) + cost
+        events.append((busy[kind] + 1.0, stream, place, kind))
+        plan.append(("start", stream) + stages[place] + (now,))
+
+    for stream in range(streams):
+        launch(1.0 * stream, stream, 0)
+    now = 0.0
+    while events:
+        event = min(events)
+        events.remove(event)
+        when, stream, place, kind = event
+        now = max(now + 0.3, when)
+        plan.append(("wait", stream) + stages[place] + (now,))
+        flying[kind] -= 1
+        if waiting[kind]:
+            launch(now, *waiting[kind].pop(0))
+        if place + 1 < len(stages):
+            launch(now, stream, place + 1)
+    return plan
 
 
 def normalize(values):
@@ -61,7 +109,7 @@
 
 
 def layer_kernel(
-    orders, tokens_ref, cot_ref, column_ref, line_ref, cos_ref, sin_ref, weights_hbm, out_ref, tokens_out,
+    orders, tokens_ref, cot_ref, lengths_ref, positions_ref, weights_hbm, out_ref, tokens_out,
     weights, normed, gout, norm_in, gout_in, mean_ref, scale_ref, linear, lin_send, lin_in, attn_send, attn_in,
     lhs_ref, small, back, back_send, acc, outgoing, incoming, w_sem, y_send, y_recv, send_sem, recv_sem,
 ):
@@ -78,6 +126,7 @@
     bit_of = [(me // (1 << bit)) % 2 for bit in range(steps)]
     peer_of = [me + (1 - 2 * bit_of[bit]) * (1 << bit) for bit in range(steps)]
     others = range(1, shards)
+    plan = exchange_plan(orders, halves)
 
     fetch = pltpu.make_async_copy(weights_hbm, weights, w_sem)
     fetch.start()
@@ -112,7 +161,8 @@
         @pl.loop(0, chunk // group)
         def masked(t):
             at = pl.ds(pl.multiple_of(part * chunk + t * group, group), group)
-            live = (column_ref[at, :] >= 0).astype(jnp.float32)
+            row = part * chunk + t * group + lax.broadcasted_iota(jnp.int32, (group, 1), 0)
+            live = jnp.where(segment_slots(lengths_ref, row) >= 0.0, 1.0, 0.0)
             for p in range(shards):
                 value = cot_ref[at, p * slab : (p + 1) * slab].astype(jnp.float32)
                 gout[p, at, :] = (value * live).astype(jnp.bfloat16)
@@ -160,6 +210,7 @@
         linear[:, i * head_size : (i + 1) * head_size] = dot(normed[shard], weights[i])
     linear[:, 3 * head_size :] = dot(gout[shard], weights[3])
 
+    cosine, sine = rotary_tables(positions_ref)
     lin_copies, attn_copies = {}, {}
 
     def attn_partial(part):
@@ -198,8 +249,9 @@
             lin_copies[part, k].wait_recv()
             linear[parts[part], : 3 * head_size] += lin_in[k - 1, parts[part], :].astype(jnp.float32)
 
-    cosine, sine = cos_ref[...], sin_ref[...]
-    same = column_ref[...] == line_ref[0:1, :]
+    same = segment_slots(lengths_ref, lax.broadcasted_iota(jnp.int32, (capacity, 1), 0)) == segment_slots(
+        lengths_ref, lax.broadcasted_iota(jnp.int32, (1, capacity), 1)
+    )
     score_scale = 1.0 / math.sqrt(HD)
     saved = []
     for h in range(heads):
@@ -282,13 +334,14 @@
             slice_gradient(k, keep)
             back_copies.append(across(10, k, -1, back_send.at[k - 1], back.at[shard]))
 
-    def token_gradients():
-        for copy in back_copies:
-            copy.wait_recv()
-
-        @pl.loop(0, capacity // group)
+    def token_gradients(number):
+        if number == 0:
+            for copy in back_copies:
+                copy.wait_recv()
+
+        @pl.loop(0, chunk // 2 // group)
         def piece(t):
-            at = pl.ds(pl.multiple_of(t * group, group), group)
+            at = pl.ds(pl.multiple_of(number * (chunk // 2) + t * group, group), group)
             scale = scale_ref[at, 0:1]
             normal = (tokens_ref[at, :].astype(jnp.float32) - mean_ref[at, 0:1]) * scale
             grad = jnp.concatenate([back[p, at, :] for p in range(shards)], axis=1).astype(jnp.float32)
@@ -336,61 +389,75 @@
         def kept(t):
             acc[stream, pl.ds(pl.multiple_of(t * TILE, TILE), TILE), :] = term(stream, mine * half + t * TILE)
 
+    def combine(stream, step):
+        copies[0, stream, step - 1].wait_recv()
+        got = starts[step - 1]
+        base = offsets[stream, step - 1] - offsets[stream, 0]
+        if step == steps:
+            half = halves[steps - 1]
+            place = pl.ds(pl.multiple_of(stream * rows + offsets[stream, steps - 1], half), half)
+            value = acc[stream, pl.ds(pl.multiple_of(base, half), half), :]
+            other = incoming[stream, pl.ds(got, half), :]
+            out_ref[place, :] = (value + other.astype(jnp.float32)).astype(jnp.bfloat16)
+            return
+        half = halves[step]
+        size = min(half, 192)
+        mine = bit_of[orders[stream][step]]
+        go, stay = (1 - mine) * half, mine * half
+
+        @pl.loop(0, half // size)
+        def leaving(t):
+            at = pl.multiple_of(t * size, size)
+            value = acc[stream, pl.ds(pl.multiple_of(base + go + at, size), size), :]
+            other = incoming[stream, pl.ds(pl.multiple_of(got + go + at, size), size), :]
+            outgoing[stream, pl.ds(pl.multiple_of(starts[step] + at, size), size), :] = (
+                value + other.astype(jnp.float32)
+            ).astype(jnp.bfloat16)
+
+        offsets[stream, step] = offsets[stream, step - 1] + stay
+
+    def combine_kept(stream, step):
+        got = starts[step - 1]
+        base = offsets[stream, step - 1] - offsets[stream, 0]
+        half = halves[step]
+        size = min(half, 192)
+        stay = bit_of[orders[stream][step]] * half
+
+        @pl.loop(0, half // size)
+        def kept(t):
+            at = pl.multiple_of(t * size, size)
+            where = pl.ds(pl.multiple_of(base + stay + at, size), size)
+            other = incoming[stream, pl.ds(pl.multiple_of(got + stay + at, size), size), :]
+            acc[stream, where, :] = acc[stream, where, :] + other.astype(jnp.float32)
+
     return_gradients()
-
-    for step in range(1, steps + 1):
-        for stream in range(streams):
-            copies[0, stream, step - 1].wait_recv()
-            got = starts[step - 1]
-            base = offsets[stream, step - 1] - offsets[stream, 0]
-            if step < steps:
-                half = halves[step]
-                size = min(half, 192)
-                mine = bit_of[orders[stream][step]]
-                go, stay = (1 - mine) * half, mine * half
-
-                @pl.loop(0, half // size)
-                def leaving(t):
-                    at = pl.multiple_of(t * size, size)
-                    value = acc[stream, pl.ds(pl.multiple_of(base + go + at, size), size), :]
-                    other = incoming[stream, pl.ds(pl.multiple_of(got + go + at, size), size), :]
-                    outgoing[stream, pl.ds(pl.multiple_of(starts[step] + at, size), size), :] = (
-                        value + other.astype(jnp.float32)
-                    ).astype(jnp.bfloat16)
-
-                place = pl.ds(starts[step], half)
-                copies[0, stream, step] = exchange(
-                    0, stream, step, outgoing.at[stream, place], incoming.at[stream, place]
-                )
-
-                @pl.loop(0, half // size)
-                def kept(t):
-                    at = pl.multiple_of(t * size, size)
-                    where = pl.ds(pl.multiple_of(base + stay + at, size), size)
-                    other = incoming[stream, pl.ds(pl.multiple_of(got + stay + at, size), size), :]
-                    acc[stream, where, :] = acc[stream, where, :] + other.astype(jnp.float32)
-
-                offsets[stream, step] = offsets[stream, step - 1] + stay
+    finish = plan[-1][-1]
+    pieces = [(0.5 + 0.1 * number) * finish for number in range(4)]
+    behind = []
+    for action, stream, phase, step, when in plan:
+        if action == "start":
+            if phase == 0 and step == 0:
+                continue
+            if phase == 0:
+                place = pl.ds(starts[step], halves[step])
+                source, target = outgoing.at[stream, place], incoming.at[stream, place]
             else:
-                half = halves[steps - 1]
-                place = pl.ds(pl.multiple_of(stream * rows + offsets[stream, steps - 1], half), half)
-                value = acc[stream, pl.ds(pl.multiple_of(base, half), half), :]
-                other = incoming[stream, pl.ds(got, half), :]
-                out_ref[place, :] = (value + other.astype(jnp.float32)).astype(jnp.bfloat16)
-                copies[1, stream, steps - 1] = exchange(
-                    1, stream, steps - 1, out_ref.at[place], out_ref.at[place]
-                )
-
-    token_gradients()
-
-    for step in reversed(range(steps - 1)):
-        for stream in range(streams):
-            copies[1, stream, step + 1].wait_recv()
-            half = halves[step]
-            place = pl.ds(pl.multiple_of(stream * rows + offsets[stream, step], half), half)
-            copies[1, stream, step] = exchange(1, stream, step, out_ref.at[place], out_ref.at[place])
-    for stream in range(streams):
-        copies[1, stream, 0].wait_recv()
+                place = pl.ds(pl.multiple_of(stream * rows + offsets[stream, step], halves[step]), halves[step])
+                source, target = out_ref.at[place], out_ref.at[place]
+            copies[phase, stream, step] = exchange(phase, stream, step, source, target)
+        else:
+            for job in behind:
+                combine_kept(*job)
+            behind = []
+            while pieces and when > pieces[0]:
+                token_gradients(4 - len(pieces))
+                pieces.pop(0)
+            if phase == 0:
+                combine(stream, step + 1)
+                if step + 1 < steps:
+                    behind.append((stream, step + 1))
+            else:
+                copies[phase, stream, step].wait_recv()
     for copy in copies.values():
         copy.wait_send()
     for copy in started:
@@ -402,13 +469,12 @@
     slab, head_size = weights.shape[1:]
     shards = lax.axis_size("fsdp")
     steps = lax.axis_size("dp").bit_length() - 1
-    streams = 4 if (slab >> steps) % 16 == 0 else 2
+    streams = next(n for n in (8, 4, 2, 1) if (4 * slab // n >> steps) % 16 == 0)
     rows = 4 * slab // streams
     plain = list(range(steps))
     turned = plain[:1] + plain[2:] + plain[1:2]
-    orders = [turned] + [plain] * (streams - 1)
+    orders = [turned] * (streams // 8) + [plain] * (streams - streams // 8)
     moved = rows - (rows >> steps)
-    column, line, cosine, sine = side_tables(lengths, positions, capacity)
     vmem = pl.BlockSpec(memory_space=pltpu.VMEM)
     half = jnp.bfloat16
     summed, grad_tokens = pl.pallas_call(
@@ -417,7 +483,7 @@
             jax.ShapeDtypeStruct((4 * slab, head_size), half),
             jax.ShapeDtypeStruct((capacity, width), half),
         ),
-        in_specs=[vmem] * 6 + [pl.BlockSpec(memory_space=pl.ANY)],
+        in_specs=[vmem, vmem, pl.BlockSpec(memory_space=pltpu.SMEM), vmem, pl.BlockSpec(memory_space=pl.ANY)],
         out_specs=(vmem, vmem),
         scratch_shapes=[
             pltpu.VMEM((4, slab, head_size), half),
@@ -449,7 +515,7 @@
             collective_id=0, has_side_effects=True, vmem_limit_bytes=62 * 1024 * 1024
         ),
         cost_estimate=pl.CostEstimate(flops=4 * 10**9, bytes_accessed=10**8, transcendentals=10**5),
-    )(tokens, cotangent, column, line, cosine, sine, weights)
+    )(tokens, cotangent, lengths, positions, weights)
     return (grad_tokens, summed.reshape(weights.shape).astype(jnp.float32))
 
 

time: 205 us -> 200 us (0.976)
  other arithmetic: 12.6 us -> 8.82 us
  local copies, waits for them, and re-layouts: 3.59 us -> 1.41 us
    slice x2 -> x0, local copies, waits for them, and re-layouts: 2.19 us -> none  [the longest x1 1.42 us: side_tables(): lengths[0, 2]]
where the time goes in v2:
time: 200 us; the launch traced here: 199 us
  Pallas kernels  188 us (94%)
  other arithmetic  8.82 us (4%)
    pallas_call x1, Pallas kernels, per_device(): pl.pallas_call(functools.partial(layer_kernel, orders), out_shape=(jax.Sh...  188 us
    convert_element_type x1, other arithmetic, per_device(): return (grad_tokens, summed.reshape(weights.shape).astype(jnp.float32))  8.82 us

profile of v2, /device:TPU:0, one launch (start us, length us, event | category | flops | bytes accessed | tf_op | source)
XLA Modules:
  0.0 198.6 jit_solution(5619749747392194295)
XLA Ops:
  0.6 187.7 %shard_map.68 = (bf16[12288,256]{1,0:T(8,128)(2,1)}, bf16[192,6144]{1,0:T(8,128)(2,1)}) custom-call(bf16[192,6144]{1,0:T(8,128)(2,1)} %tokens_ref.1, bf16[192,6144]{1,0:T(8,128)(2,1)} %cot_ref.1, s32[1,3]{1,0:T(1,128)} %lengths_ref.1, s32[2,192]{1,0:T(2,128)} %positions_ref.1, bf16[4,3072,256]{2,1,0:T(8,128)(2,1)} %weights_hbm.1), custom_call_target="tpu_custom_call" | custom-call | flops 4000000000 | bytes 100000000 | tf_op jit(solution)/shard_map/pallas_call | solution.py:480
  188.3 0.0 copy-start
  188.3 8.8 %convert.1 = f32[4,3072,256]{2,1,0:T(8,128)} convert(bf16[4,3072,256]{2,1,0:T(8,128)(2,1)} %bitcast.2) | non-fusion elementwise | flops 3145728 | bytes 18874368 | tf_op jit(solution)/shard_map/convert_element_type | solution.py:519
  197.2 0.0 copy-done
  197.2 1.4 copy.8
Async XLA Ops:
  188.3 8.8 %copy-start = (bf16[192,6144]{1,0:T(8,128)(2,1)S(1)}, bf16[192,6144]{1,0:T(8,128)(2,1)}, u32[]{:S(2)}) copy-start(bf16[192,6144]{1,0:T(8,128)(2,1)} %get-tuple-element.8) | copy-start | bytes 7077892

commit v3 on v2

--- a/solution.py
+++ b/solution.py
@@ -9,7 +9,8 @@
 from jax.sharding import PartitionSpec as P
 
 HD = 128
-TILE = 256
+TILE = 384
+CORES = 2
 
 EPS = 1e-06
 rope_base = 100.0
@@ -43,29 +44,25 @@
 
 def exchange_plan(orders, halves):
     streams, steps = len(orders), len(halves)
-    stages = [(0, s) for s in range(steps)] + [(1, s) for s in reversed(range(steps))]
-    link = lambda bit: min(bit, 2)
-    busy = {0: 0.0, 1: 0.0, 2: 0.0}
-    flying = {0: 0, 1: 0, 2: 0}
-    waiting = {0: [], 1: [], 2: []}
-    depth = {0: streams, 1: 2, 2: 2}
+    stages = [(0, s) for s in range(steps)] + [(1, s) for s in reversed(range(steps))] + [(1, steps)]
+    busy, flying, waiting = [0.0] * 4, [0] * 4, [[], [], [], []]
+    price = [0.25, 1.0, 1.0, 2.0]
     events, plan = [], []
 
     def launch(now, stream, place):
         step = stages[place][1]
-        bit = orders[stream][step]
-        kind = link(bit)
-        if flying[kind] >= depth[kind]:
+        kind = min(orders[stream][step], 3) if step < steps else 0
+        if flying[kind] >= 3:
             waiting[kind].append((stream, place))
             return
         flying[kind] += 1
-        cost = halves[step] * 0.0114 * (0.2 if bit == 0 else 1.0 if bit < 3 else 1.4)
-        busy[kind] = max(busy[kind], now) + cost
+        size = halves[step] if step < steps else 2 * halves[0]
+        busy[kind] = max(busy[kind], now) + size * 0.0114 * price[kind]
         events.append((busy[kind] + 1.0, stream, place, kind))
         plan.append(("start", stream) + stages[place] + (now,))
 
     for stream in range(streams):
-        launch(1.0 * stream, stream, 0)
+        launch(0.7 * stream, stream, 0)
     now = 0.0
     while events:
         event = min(events)
@@ -118,25 +115,28 @@
     shards = normed.shape[0]
     heads = head_size // HD
     me = lax.axis_index("dp")
-    shard = lax.axis_index("fsdp")
+    core = me % CORES
+    shard = lax.axis_index("fsdp") * CORES + core
     streams, steps = len(orders), len(orders[0])
     rows = 4 * slab // streams
     halves = [rows >> (s + 1) for s in range(steps)]
     starts = [rows - 2 * halves[s] for s in range(steps)]
-    bit_of = [(me // (1 << bit)) % 2 for bit in range(steps)]
-    peer_of = [me + (1 - 2 * bit_of[bit]) * (1 << bit) for bit in range(steps)]
+    bit_of = [(me // (1 << bit)) % 2 for bit in range(steps + 1)]
+    peer_of = [me + (1 - 2 * bit_of[bit]) * (1 << bit) for bit in range(steps + 1)]
     others = range(1, shards)
     plan = exchange_plan(orders, halves)
 
-    fetch = pltpu.make_async_copy(weights_hbm, weights, w_sem)
+    def member(offset):
+        index = (shard + shards + offset) % shards
+        return {"dp": me - core + index % CORES, "fsdp": index // CORES}
+
+    fetch = pltpu.make_async_copy(weights_hbm.at[:, pl.ds(pl.multiple_of(core * slab, slab), slab)], weights, w_sem)
     fetch.start()
     barrier = pltpu.get_barrier_semaphore()
-    for bit in range(steps):
+    for bit in range(1, steps + 1):
         pl.semaphore_signal(barrier, inc=1, device_id={"dp": peer_of[bit]}, device_id_type=pl.DeviceIdType.MESH)
     for k in others:
-        pl.semaphore_signal(
-            barrier, inc=1, device_id={"fsdp": (shard + k) % shards}, device_id_type=pl.DeviceIdType.MESH
-        )
+        pl.semaphore_signal(barrier, inc=1, device_id=member(k), device_id_type=pl.DeviceIdType.MESH)
 
     started = []
 
@@ -146,7 +146,7 @@
             dst_ref=target,
             send_sem=y_send.at[kind, k],
             recv_sem=y_recv.at[kind, k],
-            device_id={"fsdp": (shard + shards + direction * k) % shards},
+            device_id=member(direction * k),
             device_id_type=pl.DeviceIdType.MESH,
         )
         copy.start()
@@ -186,13 +186,13 @@
     def send_gout(part):
         for k in others:
             gout_copies[part, k] = across(
-                part, k, 1, gout.at[(shard + k) % shards, parts[part]], gout_in.at[k - 1, parts[part]]
+                part, k, 1, gout.at[(shard + k) % shards, parts[part]], gout_in.at[part, k - 1]
             )
 
     def send_norm(part):
         for k in others:
             norm_copies[part, k] = across(
-                2 + part, k, 1, normed.at[(shard + k) % shards, parts[part]], norm_in.at[k - 1, parts[part]]
+                2 + part, k, 1, normed.at[(shard + k) % shards, parts[part]], norm_in.at[part, k - 1]
             )
 
     mask_cotangent(0)
@@ -213,24 +213,25 @@
     cosine, sine = rotary_tables(positions_ref)
     lin_copies, attn_copies = {}, {}
 
+    apart = (shards - 1, chunk, -1)
+    joined = ((shards - 1) * chunk, slab)
+
     def attn_partial(part):
         for k in others:
             gout_copies[part, k].wait_recv()
-            attn_send[k - 1, parts[part], :] = dot(gout_in[k - 1, parts[part], :], weights[3]).astype(jnp.bfloat16)
-            attn_copies[part, k] = across(
-                4 + part, k, -1, attn_send.at[k - 1, parts[part]], attn_in.at[k - 1, parts[part]]
-            )
+        partial = dot(gout_in[part].reshape(joined), weights[3])
+        attn_send[part] = partial.astype(jnp.bfloat16).reshape(apart)
+        for k in others:
+            attn_copies[part, k] = across(4 + part, k, -1, attn_send.at[part, k - 1], attn_in.at[part, k - 1])
 
     def lin_partial(part):
         for k in others:
             norm_copies[part, k].wait_recv()
-            for i in range(3):
-                lin_send[k - 1, parts[part], i * head_size : (i + 1) * head_size] = dot(
-                    norm_in[k - 1, parts[part], :], weights[i]
-                ).astype(jnp.bfloat16)
-            lin_copies[part, k] = across(
-                6 + part, k, -1, lin_send.at[k - 1, parts[part]], lin_in.at[k - 1, parts[part]]
-            )
+        for i in range(3):
+            partial = dot(norm_in[part].reshape(joined), weights[i])
+            lin_send[part, :, :, i * head_size : (i + 1) * head_size] = partial.astype(jnp.bfloat16).reshape(apart)
+        for k in others:
+            lin_copies[part, k] = across(6 + part, k, -1, lin_send.at[part, k - 1], lin_in.at[part, k - 1])
 
     attn_partial(0)
     lin_partial(0)
@@ -240,14 +241,14 @@
         @pl.loop(0, slab // TILE)
         def turn(t):
             at = pl.ds(pl.multiple_of(t * TILE, TILE), TILE)
-            whole = jnp.concatenate([own[shard, :, at]] + [arrived[k - 1, :, at] for k in others], axis=0)
+            whole = jnp.concatenate([own[shard, :, at]] + [arrived[part, k - 1, :, at] for k in others for part in range(2)], axis=0)
             lhs_ref[pl.ds(pl.multiple_of(base + t * TILE, TILE), TILE), :] = whole.T
 
     transpose_into(0, normed, norm_in)
     for part in range(2):
         for k in others:
             lin_copies[part, k].wait_recv()
-            linear[parts[part], : 3 * head_size] += lin_in[k - 1, parts[part], :].astype(jnp.float32)
+            linear[parts[part], : 3 * head_size] += lin_in[part, k - 1].astype(jnp.float32)
 
     same = segment_slots(lengths_ref, lax.broadcasted_iota(jnp.int32, (capacity, 1), 0)) == segment_slots(
         lengths_ref, lax.broadcasted_iota(jnp.int32, (1, capacity), 1)
@@ -280,7 +281,7 @@
     for part in range(2):
         for k in others:
             attn_copies[part, k].wait_recv()
-            linear[parts[part], 3 * head_size :] += attn_in[k - 1, parts[part], :].astype(jnp.float32)
+            linear[parts[part], 3 * head_size :] += attn_in[part, k - 1].astype(jnp.float32)
 
     for h in range(heads):
         normals, queries, keys, values, prob, prob_t = saved[h]
@@ -307,32 +308,30 @@
         for k in others
     ]
 
-    def slice_gradient(slot, store):
+    def slice_gradient(first, count, store):
         @pl.loop(0, slab // TILE)
         def tile(t):
             at = pl.ds(pl.multiple_of(t * TILE, TILE), TILE)
-            total = sum(
-                dot_nt(small[i, slot * capacity : (slot + 1) * capacity, :], weights[i, at, :]) for i in range(3)
-            )
+            total = sum(dot_nt(small[i, first : first + count, :], weights[i, at, :]) for i in range(3))
             store(at, total.astype(jnp.bfloat16))
 
     def own_slice(at, value):
         back[shard, :, at] = value
 
-    slice_gradient(0, own_slice)
+    slice_gradient(0, capacity, own_slice)
     for copy in arrivals:
         copy.wait_recv()
 
     back_copies = []
 
     def return_gradients():
-        for k in others:
-
-            def keep(at, value):
-                back_send[k - 1, :, at] = value
-
-            slice_gradient(k, keep)
-            back_copies.append(across(10, k, -1, back_send.at[k - 1], back.at[shard]))
+        def keep(at, value):
+            back_send[:, at] = value
+
+        slice_gradient(capacity, (shards - 1) * capacity, keep)
+        for k in others:
+            own = pl.ds((k - 1) * capacity, capacity)
+            back_copies.append(across(10, k, -1, back_send.at[own], back.at[shard]))
 
     def token_gradients(number):
         if number == 0:
@@ -359,7 +358,7 @@
             dst_ref=target,
             send_sem=send_sem.at[phase, stream, step],
             recv_sem=recv_sem.at[phase, stream, step],
-            device_id={"dp": peer_of[orders[stream][step]]},
+            device_id={"dp": peer_of[orders[stream][step] if step < steps else 0]},
             device_id_type=pl.DeviceIdType.MESH,
         )
         copy.start()
@@ -367,6 +366,12 @@
 
     copies = {}
     offsets = {}
+    early = [item[1] for item in plan[: next(n for n, item in enumerate(plan) if item[0] == "wait")]]
+
+    def start_first(stream):
+        place = pl.ds(0, halves[0])
+        copies[0, stream, 0] = exchange(0, stream, 0, outgoing.at[stream, place], incoming.at[stream, place])
+
     for stream in range(streams):
         half = halves[0]
         mine = bit_of[orders[stream][0]]
@@ -376,12 +381,11 @@
             value = term(stream, (1 - mine) * half + t * TILE)
             outgoing[stream, pl.ds(pl.multiple_of(t * TILE, TILE), TILE), :] = value.astype(jnp.bfloat16)
 
-        copies[0, stream, 0] = exchange(
-            0, stream, 0, outgoing.at[stream, pl.ds(0, half)], incoming.at[stream, pl.ds(0, half)]
-        )
+        if stream in early:
+            start_first(stream)
         offsets[stream, 0] = mine * half
 
-    for stream in range(streams):
+    def first_kept(stream):
         half = halves[0]
         mine = bit_of[orders[stream][0]]
 
@@ -395,7 +399,7 @@
         base = offsets[stream, step - 1] - offsets[stream, 0]
         if step == steps:
             half = halves[steps - 1]
-            place = pl.ds(pl.multiple_of(stream * rows + offsets[stream, steps - 1], half), half)
+            place = pl.ds(pl.multiple_of((core * streams + stream) * rows + offsets[stream, steps - 1], half), half)
             value = acc[stream, pl.ds(pl.multiple_of(base, half), half), :]
             other = incoming[stream, pl.ds(got, half), :]
             out_ref[place, :] = (value + other.astype(jnp.float32)).astype(jnp.bfloat16)
@@ -437,12 +441,16 @@
     for action, stream, phase, step, when in plan:
         if action == "start":
             if phase == 0 and step == 0:
+                if stream not in early:
+                    start_first(stream)
                 continue
             if phase == 0:
                 place = pl.ds(starts[step], halves[step])
                 source, target = outgoing.at[stream, place], incoming.at[stream, place]
             else:
-                place = pl.ds(pl.multiple_of(stream * rows + offsets[stream, step], halves[step]), halves[step])
+                size = halves[step] if step < steps else rows
+                shift = offsets[stream, step] if step < steps else 0
+                place = pl.ds(pl.multiple_of((core * streams + stream) * rows + shift, size), size)
                 source, target = out_ref.at[place], out_ref.at[place]
             copies[phase, stream, step] = exchange(phase, stream, step, source, target)
         else:
@@ -453,6 +461,8 @@
                 token_gradients(4 - len(pieces))
                 pieces.pop(0)
             if phase == 0:
+                if step == 0:
+                    first_kept(stream)
                 combine(stream, step + 1)
                 if step + 1 < steps:
                     behind.append((stream, step + 1))
@@ -466,21 +476,22 @@
 
 def per_device(tokens, cotangent, lengths, positions, weights):
     capacity, width = tokens.shape
-    slab, head_size = weights.shape[1:]
-    shards = lax.axis_size("fsdp")
-    steps = lax.axis_size("dp").bit_length() - 1
+    slab, head_size = weights.shape[1] // CORES, weights.shape[2]
+    shards = lax.axis_size("fsdp") * CORES
+    steps = lax.axis_size("dp").bit_length() - 2
     streams = next(n for n in (8, 4, 2, 1) if (4 * slab // n >> steps) % 16 == 0)
     rows = 4 * slab // streams
-    plain = list(range(steps))
-    turned = plain[:1] + plain[2:] + plain[1:2]
+    plain = list(range(1, steps + 1))
+    turned = plain[1:] + plain[:1]
     orders = [turned] * (streams // 8) + [plain] * (streams - streams // 8)
     moved = rows - (rows >> steps)
+    chunk = capacity // 2
     vmem = pl.BlockSpec(memory_space=pltpu.VMEM)
     half = jnp.bfloat16
     summed, grad_tokens = pl.pallas_call(
         functools.partial(layer_kernel, orders),
         out_shape=(
-            jax.ShapeDtypeStruct((4 * slab, head_size), half),
+            jax.ShapeDtypeStruct((CORES * 4 * slab, head_size), half),
             jax.ShapeDtypeStruct((capacity, width), half),
         ),
         in_specs=[vmem, vmem, pl.BlockSpec(memory_space=pltpu.SMEM), vmem, pl.BlockSpec(memory_space=pl.ANY)],
@@ -489,34 +500,35 @@
             pltpu.VMEM((4, slab, head_size), half),
             pltpu.VMEM((shards, capacity, slab), half),
             pltpu.VMEM((shards, capacity, slab), half),
-            pltpu.VMEM((shards - 1, capacity, slab), half),
-            pltpu.VMEM((shards - 1, capacity, slab), half),
+            pltpu.VMEM((2, shards - 1, chunk, slab), half),
+            pltpu.VMEM((2, shards - 1, chunk, slab), half),
             pltpu.VMEM((capacity, HD), jnp.float32),
             pltpu.VMEM((capacity, HD), jnp.float32),
             pltpu.VMEM((capacity, 4 * head_size), jnp.float32),
-            pltpu.VMEM((shards - 1, capacity, 3 * head_size), half),
-            pltpu.VMEM((shards - 1, capacity, 3 * head_size), half),
-            pltpu.VMEM((shards - 1, capacity, head_size), half),
-            pltpu.VMEM((shards - 1, capacity, head_size), half),
+            pltpu.VMEM((2, shards - 1, chunk, 3 * head_size), half),
+            pltpu.VMEM((2, shards - 1, chunk, 3 * head_size), half),
+            pltpu.VMEM((2, shards - 1, chunk, head_size), half),
+            pltpu.VMEM((2, shards - 1, chunk, head_size), half),
             pltpu.VMEM((2 * slab, shards * capacity), half),
             pltpu.VMEM((4, shards * capacity, head_size), half),
             pltpu.VMEM((shards, capacity, slab), half),
-            pltpu.VMEM((shards - 1, capacity, slab), half),
+            pltpu.VMEM(((shards - 1) * capacity, slab), half),
             pltpu.VMEM((streams, rows // 2, head_size), jnp.float32),
             pltpu.VMEM((streams, moved, head_size), half),
             pltpu.VMEM((streams, moved, head_size), half),
             pltpu.SemaphoreType.DMA,
             pltpu.SemaphoreType.DMA((11, shards)),
             pltpu.SemaphoreType.DMA((11, shards)),
-            pltpu.SemaphoreType.DMA((2, streams, steps)),
-            pltpu.SemaphoreType.DMA((2, streams, steps)),
+            pltpu.SemaphoreType.DMA((2, streams, steps + 1)),
+            pltpu.SemaphoreType.DMA((2, streams, steps + 1)),
         ],
         compiler_params=pltpu.CompilerParams(
             collective_id=0, has_side_effects=True, vmem_limit_bytes=62 * 1024 * 1024
         ),
         cost_estimate=pl.CostEstimate(flops=4 * 10**9, bytes_accessed=10**8, transcendentals=10**5),
     )(tokens, cotangent, lengths, positions, weights)
-    return (grad_tokens, summed.reshape(weights.shape).astype(jnp.float32))
+    halved = summed.reshape(CORES, 4, slab, head_size).astype(jnp.float32)
+    return (grad_tokens, jnp.transpose(halved, (1, 0, 2, 3)).reshape(weights.shape))
 
 
 def solution(mesh):

time: 200 us -> 196 us (0.980)
  Pallas kernels: 188 us -> 175 us
  local copies, waits for them, and re-layouts: 1.41 us -> 11.7 us
    pallas_call x1, Pallas kernels: 188 us -> 175 us  [per_device(): pl.pallas_call(functools.partial(layer_kernel, orders), out_shape=(jax.Sh...]
    reshape x0 -> x1, local copies, waits for them, and re-layouts: none -> 10.3 us  [per_device(): jnp.transpose(halved, (1, 0, 2, 3)).reshape(weights.shape)]
    convert_element_type x1 -> x0, other arithmetic: 8.82 us -> none  [per_device(): return (grad_tokens, summed.reshape(weights.shape).astype(jnp.float32))]
    reshape x0 -> x1, other arithmetic: none -> 8.48 us  [per_device(): jnp.transpose(halved, (1, 0, 2, 3)).reshape(weights.shape)]
where the time goes in v3:
time: 196 us
  Pallas kernels  175 us (89%)
  local copies, waits for them, and re-layouts  11.7 us (6%)
  other arithmetic  8.48 us (4%)
    pallas_call x1, Pallas kernels, per_device(): pl.pallas_call(functools.partial(layer_kernel, orders), out_shape=(jax.Sh...  175 us
    reshape x1, local copies, waits for them, and re-layouts, per_device(): jnp.transpose(halved, (1, 0, 2, 3)).reshape(weights.shape)  10.3 us
    reshape x1, other arithmetic, per_device(): jnp.transpose(halved, (1, 0, 2, 3)).reshape(weights.shape)  8.48 us

profile of v3, /device:TPU:0, one launch (start us, length us, event | category | flops | bytes accessed | tf_op | source)
XLA Modules:
  0.0 195.6 jit_solution(10851043297771951398)
XLA Ops:
  0.6 174.8 %shard_map.68 = (bf16[12288,256]{1,0:T(8,128)(2,1)}, bf16[192,6144]{1,0:T(8,128)(2,1)}) custom-call(bf16[192,6144]{1,0:T(8,128)(2,1)} %tokens_ref.1, bf16[192,6144]{1,0:T(8,128)(2,1)} %cot_ref.1, s32[1,3]{1,0:T(1,128)} %lengths_ref.1, s32[2,192]{1,0:T(2,128)} %positions_ref.1, bf16[4,3072,256]{2,1,0:T(8,128)(2,1)} %weights_hbm.1), custom_call_target="tpu_custom_call" | custom-call | flops 4000000000 | bytes 100000000 | tf_op jit(solution)/shard_map/pallas_call | solution.py:491
  175.4 8.5 %convert_bitcast_fusion = f32[4,2,1536,256]{3,2,0,1:T(8,128)} fusion(bf16[2,4,1536,256]{3,2,1,0:T(8,128)(2,1)} %bitcast.6), kind=kLoop, calls=%fused_computation | loop fusion | flops 3145728 | bytes 18874368 | tf_op jit(solution)/shard_map/reshape | solution.py:531
  183.9 0.0 copy-start
  183.9 10.3 %copy.7 = f32[4,2,1536,256]{3,2,1,0:T(8,128)} copy(f32[4,2,1536,256]{3,2,0,1:T(8,128)} %convert_bitcast_fusion) | data formatting | bytes 25165824 | tf_op jit(solution)/shard_map/reshape | solution.py:531
  194.2 0.0 copy-done
  194.2 1.4 copy.9
Async XLA Ops:
  183.9 10.3 %copy-start = (bf16[192,6144]{1,0:T(8,128)(2,1)S(1)}, bf16[192,6144]{1,0:T(8,128)(2,1)}, u32[]{:S(2)}) copy-start(bf16[192,6144]{1,0:T(8,128)(2,1)} %get-tuple-element.8) | copy-start | bytes 7077892

commit v4 on v3

--- a/solution.py
+++ b/solution.py
@@ -393,13 +393,19 @@
         def kept(t):
             acc[stream, pl.ds(pl.multiple_of(t * TILE, TILE), TILE), :] = term(stream, mine * half + t * TILE)
 
+    def placed(stream, shift):
+        if rows > slab:
+            return (core * streams + stream) * rows + shift
+        weight = stream * rows // slab
+        return (weight * CORES + core) * slab + stream * rows % slab + shift
+
     def combine(stream, step):
         copies[0, stream, step - 1].wait_recv()
         got = starts[step - 1]
         base = offsets[stream, step - 1] - offsets[stream, 0]
         if step == steps:
             half = halves[steps - 1]
-            place = pl.ds(pl.multiple_of((core * streams + stream) * rows + offsets[stream, steps - 1], half), half)
+            place = pl.ds(pl.multiple_of(placed(stream, offsets[stream, steps - 1]), half), half)
             value = acc[stream, pl.ds(pl.multiple_of(base, half), half), :]
             other = incoming[stream, pl.ds(got, half), :]
             out_ref[place, :] = (value + other.astype(jnp.float32)).astype(jnp.bfloat16)
@@ -450,7 +456,7 @@
             else:
                 size = halves[step] if step < steps else rows
                 shift = offsets[stream, step] if step < steps else 0
-                place = pl.ds(pl.multiple_of((core * streams + stream) * rows + shift, size), size)
+                place = pl.ds(pl.multiple_of(placed(stream, shift), size), size)
                 source, target = out_ref.at[place], out_ref.at[place]
             copies[phase, stream, step] = exchange(phase, stream, step, source, target)
         else:
@@ -527,8 +533,9 @@
         ),
         cost_estimate=pl.CostEstimate(flops=4 * 10**9, bytes_accessed=10**8, transcendentals=10**5),
     )(tokens, cotangent, lengths, positions, weights)
-    halved = summed.reshape(CORES, 4, slab, head_size).astype(jnp.float32)
-    return (grad_tokens, jnp.transpose(halved, (1, 0, 2, 3)).reshape(weights.shape))
+    if rows > slab:
+        summed = jnp.transpose(summed.reshape(CORES, 4, slab, head_size), (1, 0, 2, 3))
+    return (grad_tokens, summed.reshape(weights.shape).astype(jnp.float32))
 
 
 def solution(mesh):

time: 196 us -> 186 us (0.949)
  local copies, waits for them, and re-layouts: 11.7 us -> 1.41 us
    reshape x1 -> x0, local copies, waits for them, and re-layouts: 10.3 us -> none  [per_device(): jnp.transpose(halved, (1, 0, 2, 3)).reshape(weights.shape)]
    convert_element_type x0 -> x1, other arithmetic: none -> 8.82 us  [per_device(): return (grad_tokens, summed.reshape(weights.shape).astype(jnp.float32))]
    reshape x1 -> x0, other arithmetic: 8.48 us -> none  [per_device(): jnp.transpose(halved, (1, 0, 2, 3)).reshape(weights.shape)]
where the time goes in v4:
time: 186 us
  Pallas kernels  175 us (94%)
  other arithmetic  8.82 us (5%)
    pallas_call x1, Pallas kernels, per_device(): pl.pallas_call(functools.partial(layer_kernel, orders), out_shape=(jax.Sh...  175 us
    convert_element_type x1, other arithmetic, per_device(): return (grad_tokens, summed.reshape(weights.shape).astype(jnp.float32))  8.82 us

profile of v4, /device:TPU:0, one launch (start us, length us, event | category | flops | bytes accessed | tf_op | source)
XLA Modules:
  0.0 185.7 jit_solution(10592418743374981530)
XLA Ops:
  0.6 174.8 %shard_map.68 = (bf16[12288,256]{1,0:T(8,128)(2,1)}, bf16[192,6144]{1,0:T(8,128)(2,1)}) custom-call(bf16[192,6144]{1,0:T(8,128)(2,1)} %tokens_ref.1, bf16[192,6144]{1,0:T(8,128)(2,1)} %cot_ref.1, s32[1,3]{1,0:T(1,128)} %lengths_ref.1, s32[2,192]{1,0:T(2,128)} %positions_ref.1, bf16[4,3072,256]{2,1,0:T(8,128)(2,1)} %weights_hbm.1), custom_call_target="tpu_custom_call" | custom-call | flops 4000000000 | bytes 100000000 | tf_op jit(solution)/shard_map/pallas_call | solution.py:497
  175.4 0.0 copy-start
  175.5 8.8 %convert.1 = f32[4,3072,256]{2,1,0:T(8,128)} convert(bf16[4,3072,256]{2,1,0:T(8,128)(2,1)} %bitcast.2) | non-fusion elementwise | flops 3145728 | bytes 18874368 | tf_op jit(solution)/shard_map/convert_element_type | solution.py:538
  184.3 0.0 copy-done
  184.3 1.4 copy.8
Async XLA Ops:
  175.4 8.8 %copy-start = (bf16[192,6144]{1,0:T(8,128)(2,1)S(1)}, bf16[192,6144]{1,0:T(8,128)(2,1)}, u32[]{:S(2)}) copy-start(bf16[192,6144]{1,0:T(8,128)(2,1)} %get-tuple-element.8) | copy-start | bytes 7077892
